TPU v7x, 32 devices: a whole 2x2x4 slice. The times are simulated.
32 devices in a mesh: seq: 16 (over z, y, core), tp: 2 (over x).
Axes of the slice: x: 2, y: 2, z: 4, core: 2. Of those that a mesh axis runs over, the one named last changes fastest.
Arguments:
- hidden: bfloat16 [4096, 4096], P('seq', 'tp'), may hold values from -6 to 6
- neighbours: bfloat16 [64, 256, 896], P('seq'), may hold values from -6 to 6
- enc_gain: float32 [896], replicated, may hold values from 0.25 to 1.75
- enc_w1: bfloat16 [896, 3584], P(None, 'tp'), may hold values from -0.1875 to 0.1875
- enc_w2: bfloat16 [3584, 896], P('tp'), may hold values from -0.09375 to 0.09375
- key_weight: bfloat16 [896, 4096], P(None, 'tp'), may hold values from -0.1875 to 0.1875
- value_weight: bfloat16 [896, 4096], P(None, 'tp'), may hold values from -0.1875 to 0.1875
- dec_gain: float32 [4096], replicated, may hold values from 0.25 to 1.75
- query_weight: bfloat16 [4096, 4096], P('seq', 'tp'), may hold values from -0.09375 to 0.09375
- out_weight: bfloat16 [4096, 4096], P('tp', 'seq'), may hold values from -0.09375 to 0.09375
Outputs:
- mixed: bfloat16 [4096, 4096], P('seq', 'tp')
All inputs are finite; a program needn't handle non-finite values.
Results may differ from a plain program's by a relative error of at most 0.015.
Values may be sent and summed in bfloat16 or wider, within the bound.
No kernel may reach another device: no remote copies, remote signals or barrier semaphores. Data moves between devices by JAX's collectives and lax.ppermute only.
A program may use at most 128 MiB of HBM per device.

v0:
```python
import jax
import jax.numpy as jnp
from jax import lax
from jax.sharding import PartitionSpec as P

HD = 128
M = 64
NEIGH = 2
RLEN = 128


def shifted(value, axis, by):
    devices = lax.axis_size(axis)
    pairs = [(i, i + by) for i in range(devices) if 0 <= i + by < devices]
    return lax.ppermute(value, axis, pairs)


def rms_scale(values32, gain):
    return (
        values32 * lax.rsqrt(jnp.mean(values32 * values32, axis=-1, keepdims=True) + 1e-06) * gain
    )


def feed_partial(tokens, enc_gain, first_weight, second_weight):
    enc_norm = rms_scale(tokens.astype(jnp.float32), enc_gain).astype(jnp.bfloat16)
    inner = jax.nn.relu(jnp.dot(enc_norm, first_weight, preferred_element_type=jnp.float32)).astype(
        jnp.bfloat16
    )
    return jnp.dot(inner, second_weight, preferred_element_type=jnp.float32)


def encode(batch, enc_gain, enc_w1, enc_w2):
    row_count = batch.shape[0] * batch.shape[1]
    flat = batch.reshape(row_count, batch.shape[2])
    summed = lax.psum(
        feed_partial(flat, enc_gain, enc_w1, enc_w2).astype(jnp.bfloat16), "tp"
    ).astype(jnp.float32)
    return (flat.astype(jnp.float32) + summed).astype(jnp.bfloat16)


def project_heads(encoded, weight, span_count):
    result = jnp.dot(encoded, weight, preferred_element_type=jnp.float32).astype(jnp.bfloat16)
    return result.reshape(span_count, NEIGH * RLEN, weight.shape[1] // HD, HD)


def per_device(
    hidden,
    neighbours,
    enc_gain,
    enc_w1,
    enc_w2,
    key_weight,
    value_weight,
    dec_gain,
    query_weight,
    out_weight,
):
    tok_rows = hidden.shape[0]
    span_count = neighbours.shape[0]
    earlier = shifted(neighbours[span_count - 1 :], "seq", 1)
    batch = jnp.concatenate([earlier, neighbours], axis=0)
    encoded = encode(batch, enc_gain, enc_w1, enc_w2)
    keys_all = project_heads(encoded, key_weight, span_count + 1)
    values_all = project_heads(encoded, value_weight, span_count + 1)
    features = lax.all_gather(hidden, "tp", axis=1, tiled=True)
    dec_norm = rms_scale(features.astype(jnp.float32), dec_gain).astype(jnp.bfloat16)
    query = jnp.dot(
        dec_norm,
        lax.all_gather(query_weight, "seq", axis=0, tiled=True),
        preferred_element_type=jnp.float32,
    ).astype(jnp.bfloat16)
    head_count = query.shape[1] // HD
    grouped = jnp.pad(query, ((1, M - 1), (0, 0))).reshape(span_count + 1, M, head_count, HD)
    scores = jnp.einsum(
        "cmhd,cnhd->chmn", grouped, keys_all, preferred_element_type=jnp.float32
    ) * HD ** (-0.5)
    probs = jax.nn.softmax(scores, axis=-1).astype(jnp.bfloat16)
    attn = jnp.einsum(
        "chmn,cnhd->cmhd", probs, values_all, preferred_element_type=jnp.float32
    ).astype(jnp.bfloat16)
    attn = attn.reshape((span_count + 1) * M, head_count * HD)[1 : tok_rows + 1]
    position = lax.axis_index("seq") * tok_rows + jnp.arange(tok_rows, dtype=jnp.int32)[:, None]
    attn = jnp.where(position >= M - 1, attn, jnp.zeros_like(attn))
    partial_value = jnp.dot(
        attn,
        lax.all_gather(out_weight, "seq", axis=1, tiled=True),
        preferred_element_type=jnp.float32,
    )
    branch = lax.psum_scatter(
        partial_value.astype(jnp.bfloat16), "tp", scatter_dimension=1, tiled=True
    ).astype(jnp.float32)
    return (hidden.astype(jnp.float32) + branch).astype(jnp.bfloat16)


def solution(mesh):
    placed = (
        P("seq", "tp"),
        P("seq", None, None),
        P(),
        P(None, "tp"),
        P("tp", None),
        P(None, "tp"),
        P(None, "tp"),
        P(),
        P("seq", "tp"),
        P("tp", "seq"),
    )
    return jax.shard_map(
        per_device, mesh=mesh, in_specs=placed, out_specs=P("seq", "tp"), check_vma=False
    )
```

profile of v0, /device:TPU:0, one launch (start us, length us, event | category | flops | bytes accessed | tf_op | source)
XLA Modules:
  0.0 428.7 jit_solution(5360567129774109131)
XLA Ops:
  6.5 0.0 copy-start
  6.5 0.0 copy-start.5
  6.5 0.0 all-gather.4.cloned.1.call-start
  6.5 2.0 slice.6
  8.5 3.1 collective-permute-start
  11.6 0.0 all-gather.4.cloned.1.call-update
  11.7 0.0 all-reduce.3.cloned.1.call-start
  11.7 0.9 collective-permute-done
  12.6 2.1 fusion.7
  14.8 0.0 copy-done.5
  14.8 3.6 fusion.9
  18.3 0.0 copy-done
  18.3 13.5 %convolution_convert_fusion.3 = bf16[1280,896]{1,0:T(8,128)(2,1)} fusion(bf16[1792,896]{1,0:T(8,128)(2,1)S(1)} %copy-done, bf16[1280,896]{1,0:T(8,128)(2,1)} %fusion.9, bf16[896,1792]{1,0:T(8,128)(2,1)} %param.13), kind=kOutput, calls=%fused_computation.26 | convolution fusion | flops 8226570240 | bytes 11010048 | tf_op jit(solution)/shard_map/dot_general | solution.py:29
  31.8 0.0 copy-start.2
  31.8 0.0 all-reduce.3.cloned.1.call-update
  31.9 0.0 all-gather.6.cloned.1.call-start
  31.9 0.7 all-gather.6.cloned.1.call-update
  32.6 0.0 all-gather.8.cloned.1.call-start
  32.6 0.5 all-gather.8.cloned.1.call-update
  33.2 0.2 reduce-scatter.2.cloned.1.call-start
  33.4 13.3 %all-gather.4.cloned.1.call-done = bf16[256,4096]{1,0:T(8,128)(2,1)} async-done(((bf16[256,2048]{1,0:T(8,128)(2,1)}), bf16[256,4096]{1,0:T(8,128)(2,1)}) %all-gather.4.cloned.1.call-update) | async-done | bytes 2097168 | tf_op jit(solution)/shard_map/all_gather | solution.py:65
  46.7 2.1 fusion.11
  48.8 67.5 %all-reduce.3.cloned.1.call-done = bf16[1280,896]{1,0:T(8,128)(2,1)} async-done(((bf16[1280,896]{1,0:T(8,128)(2,1)}), bf16[1280,896]{1,0:T(8,128)(2,1)}) %all-reduce.3.cloned.1.call-update) | async-done | bytes 2293776 | tf_op jit(solution)/shard_map/psum | solution.py:35
  116.3 0.0 copy-done.2
  116.3 0.0 copy-start.6
  116.3 2.4 fusion.10
  118.7 0.4 copy-done.6
  119.2 5.8 %fusion.19 = bf16[160,8,16,128]{3,1,2,0:T(8,128)(2,1)S(1)} fusion(bf16[1280,896]{1,0:T(8,128)(2,1)S(1)} %fusion.10, bf16[896,2048]{1,0:T(8,128)(2,1)S(1)} %copy-done.6), kind=kOutput, calls=%fused_computation.31 | convolution fusion | flops 4700241920 | bytes 11206656 | tf_op jit(solution)/shard_map/dot_general | solution.py:42
  125.0 0.0 copy-start.7
  125.0 4.1 copy.19
  129.1 0.0 copy-done.7
  129.1 5.8 %fusion.18 = bf16[160,8,16,128]{3,1,2,0:T(8,128)(2,1)S(1)} fusion(bf16[1280,896]{1,0:T(8,128)(2,1)S(1)} %fusion.10, bf16[896,2048]{1,0:T(8,128)(2,1)S(1)} %copy-done.7), kind=kOutput, calls=%fused_computation.30 | convolution fusion | flops 4700241920 | bytes 11206656 | tf_op jit(solution)/shard_map/dot_general | solution.py:42
  134.9 0.0 copy-start.4
  134.9 0.0 copy-start.8
  134.9 4.1 copy.20
  139.1 106.6 %all-gather.6.cloned.1.call-done = bf16[4096,2048]{1,0:T(8,128)(2,1)} async-done(((bf16[256,2048]{1,0:T(8,128)(2,1)}), bf16[4096,2048]{1,0:T(8,128)(2,1)}) %all-gather.6.cloned.1.call-update) | async-done | bytes 16777232 | tf_op jit(solution)/shard_map/all_gather | solution.py:69
  245.6 0.0 copy-done.4
  245.6 0.0 copy-done.8
  245.6 8.6 %convolution_convert_fusion.4 = bf16[256,2048]{1,0:T(8,128)(2,1)S(1)} fusion(bf16[4096,2048]{1,0:T(8,128)(2,1)} %all-gather.6.cloned.1.call-done, bf16[256,4096]{1,0:T(8,128)(2,1)S(1)} %copy-done.4, f32[4096]{0:T(1024)S(1)} %copy-done.8, f32[256]{0:T(256)S(1)} %add_rsqrt_fusion.1), kind=kOutput, calls=%fused_computation.29 | convolution fusion | flops 4299685888 | bytes 19940352 | tf_op jit(solution)/shard_map/dot_general | solution.py:67
  254.2 0.4 pad_bitcast_fusion
  254.6 0.3 copy.18
  254.9 4.6 %fusion.4 = f32[5,16,64,256]{3,2,1,0:T(8,128)S(1)} fusion(bf16[5,256,16,128]{3,2,1,0:T(8,128)(2,1)} %bitcast.37, bf16[5,64,16,128]{3,2,1,0:T(8,128)(2,1)S(1)} %bitcast.40), kind=kOutput, calls=%fused_computation.9 | convolution fusion | flops 335544320 | bytes 11796480 | tf_op jit(solution)/shard_map/cmhd,cnhd->chmn/dot_general | solution.py:74
  259.5 0.0 copy-start.3
  259.5 2.3 copy-done.3
  261.8 2.0 fusion.42
  263.8 14.6 %fusion.26 = bf16[5,64,16,128]{3,1,2,0:T(8,128)(2,1)S(1)} fusion(bf16[5,256,16,128]{3,2,1,0:T(8,128)(2,1)} %bitcast.38, f32[5,16,64]{2,1,0:T(8,128)S(1)} %fusion.42, f32[5,16,64,256]{3,2,1,0:T(8,128)} %copy-done.3), kind=kOutput, calls=%fused_computation.37 | convolution fusion | flops 342758656 | bytes 11816960 | tf_op jit(solution)/shard_map/chmn,cnhd->cmhd/dot_general | solution.py:78
  278.4 0.9 copy.17
  279.3 1.4 copy.33
  280.7 95.7 %all-gather.8.cloned.1.call-done = bf16[2048,4096]{1,0:T(8,128)(2,1)} async-done(((bf16[2048,256]{1,0:T(8,128)(2,1)}), bf16[2048,4096]{1,0:T(8,128)(2,1)}) %all-gather.8.cloned.1.call-update) | async-done | bytes 16777232 | tf_op jit(solution)/shard_map/all_gather | solution.py:86
  376.4 0.0 copy-start.1
  376.4 12.7 %convolution_convert_fusion.2 = bf16[256,4096]{1,0:T(8,128)(2,1)} fusion(bf16[2048,4096]{1,0:T(8,128)(2,1)} %all-gather.8.cloned.1.call-done, bf16[320,2048]{1,0:T(8,128)(2,1)} %bitcast.41, pred[256]{0:T(512)(128)(4,1)S(1)} %add_compare_fusion), kind=kOutput, calls=%fused_computation.13 | convolution fusion | flops 4296540160 | bytes 19923200 | tf_op jit(solution)/shard_map/dot_general | solution.py:84
  389.1 0.0 reduce-scatter.2.cloned.1.call-update
  389.1 30.1 %reduce-scatter.2.cloned.1.call-done = bf16[256,2048]{1,0:T(8,128)(2,1)} async-done(((bf16[256,4096]{1,0:T(8,128)(2,1)}), bf16[256,2048]{1,0:T(8,128)(2,1)}) %reduce-scatter.2.cloned.1.call-update) | async-done | bytes 1048592 | tf_op jit(solution)/shard_map/reduce_scatter | solution.py:89
  419.3 2.9 add_convert_fusion
  422.2 0.0 copy-done.1
  (4 shorter events, 0.0 us)
Async XLA Ops:
  6.5 11.8 %copy-start = (bf16[1792,896]{1,0:T(8,128)(2,1)S(1)}, bf16[1792,896]{1,0:T(8,128)(2,1)}, u32[]{:S(2)}) copy-start(bf16[1792,896]{1,0:T(8,128)(2,1)} %param.14) | copy-start | bytes 9633796
  6.5 8.2 %copy-start.5 = (f32[896]{0:T(1024)S(1)}, f32[896]{0:T(1024)}, u32[]{:S(2)}) copy-start(f32[896]{0:T(1024)} %param.12) | copy-start | bytes 10756
  6.5 40.2 %all-gather.4.cloned.1.call-start = ((), (), s32[]{:S(2)}) async-start(), calls=%async_computation.2 | async-start | bytes 3145728 | tf_op jit(solution)/shard_map/all_gather | solution.py:65
  8.5 4.1 collective-permute-start
  11.7 104.6 %all-reduce.3.cloned.1.call-start = ((), (), s32[]{:S(2)}) async-start(), calls=%async_computation.1 | async-start | bytes 4587520 | tf_op jit(solution)/shard_map/psum | solution.py:35
  31.8 84.5 %copy-start.2 = (bf16[4,256,896]{2,1,0:T(8,128)(2,1)S(1)}, bf16[4,256,896]{2,1,0:T(8,128)(2,1)}, u32[]{:S(2)}) copy-start(bf16[4,256,896]{2,1,0:T(8,128)(2,1)} %param.11) | copy-start | bytes 5505028
  31.9 213.8 %all-gather.6.cloned.1.call-start = ((), (), s32[]{:S(2)}) async-start(), calls=%async_computation.3 | async-start | bytes 17825792 | tf_op jit(solution)/shard_map/all_gather | solution.py:69
  32.6 343.8 %all-gather.8.cloned.1.call-start = ((), (), s32[]{:S(2)}) async-start(), calls=%async_computation.4 | async-start | bytes 17825792 | tf_op jit(solution)/shard_map/all_gather | solution.py:86
  33.2 386.1 %reduce-scatter.2.cloned.1.call-start = ((), (), s32[]{:S(2)}) async-start(), calls=%async_computation.5 | async-start | bytes 3145728 | tf_op jit(solution)/shard_map/reduce_scatter | solution.py:89
  116.3 2.9 copy-start.6
  125.0 4.1 copy-start.7
  134.9 110.7 %copy-start.4 = (bf16[256,4096]{1,0:T(8,128)(2,1)S(1)}, bf16[256,4096]{1,0:T(8,128)(2,1)}, u32[]{:S(2)}) copy-start(bf16[256,4096]{1,0:T(8,128)(2,1)} %all-gather.4.cloned.1.call-done) | copy-start | bytes 6291460
  134.9 110.7 %copy-start.8 = (f32[4096]{0:T(1024)S(1)}, f32[4096]{0:T(1024)}, u32[]{:S(2)}) copy-start(f32[4096]{0:T(1024)} %param.17) | copy-start | bytes 49156
  259.5 2.3 copy-start.3
  376.4 45.8 %copy-start.1 = (bf16[1792,896]{1,0:T(8,128)(2,1)S(1)}, bf16[1792,896]{1,0:T(8,128)(2,1)}, u32[]{:S(2)}) copy-start(bf16[1792,896]{1,0:T(8,128)(2,1)} %param.14) | copy-start | bytes 9633796
Sparse Core Ops, SparseCore 0:
  11.8 34.9 all-gather.3
  49.1 67.1 all-reduce.2
  118.7 126.8 all-gather.5
  247.9 128.5 all-gather.7
  389.2 29.9 reduce-scatter.1
where the time goes:
time: 429 us
  waiting for transfers between devices  315 us (73%)
  matrix products  65.6 us (15%)
  local copies, waits for them, and re-layouts  15.9 us (4%)
  other arithmetic  15.1 us (4%)
  between operations  13.3 us (3%)
    all_gather x1, waiting for transfers between devices, per_device(): lax.all_gather(query_weight, 'seq', axis=0, tiled=True)  107 us
    all_gather x1, waiting for transfers between devices, per_device(): lax.all_gather(out_weight, 'seq', axis=1, tiled=True)  95.7 us
    psum x1, waiting for transfers between devices, encode(): lax.psum(feed_partial(flat, enc_gain, enc_w1, enc_w2).astype(jnp.bfloat16...  67.5 us
    reduce_scatter x1, waiting for transfers between devices, per_device(): lax.psum_scatter(partial_value.astype(jnp.bfloat16), 'tp', scatter_dimens...  30.1 us
    dot_general x1, matrix products, per_device(): jnp.einsum('chmn,cnhd->cmhd', probs, values_all, preferred_element_type=j...  14.6 us
    dot_general x1, matrix products, feed_partial(): return jnp.dot(inner, second_weight, preferred_element_type=jnp.float32)  13.5 us
    all_gather x1, waiting for transfers between devices, per_device(): features = lax.all_gather(hidden, 'tp', axis=1, tiled=True)  13.3 us
    unnamed x23, local copies, waits for them, and re-layouts  13 us
  transfers between devices with their start and end apart: 6, of which 6 were waited for; matrix products, arithmetic and copies ran while one was open for 18% of the time, Pallas kernels for 0%

commit v1 on v0

v1 whole, which is shorter than its diff:
```python
import functools

import jax
import jax.numpy as jnp
from jax import lax
from jax.experimental import pallas as pl
from jax.experimental.pallas import tpu as pltpu
from jax.sharding import PartitionSpec as P

HD = 128
M = 64
KEYS = 256


def factors(count):
    core = 2 if count % 2 == 0 else 1
    y = 2 if (count // core) % 2 == 0 else 1
    return count // (core * y), y, core


def swap(value, axis, stride, size):
    count = lax.axis_size(axis)
    if size == 1:
        return value
    pairs = [(i, i + stride if (i // stride) % 2 == 0 else i - stride) for i in range(count)]
    return lax.ppermute(value, axis, pairs)


def ring(value, axis, stride):
    count = lax.axis_size(axis)
    return lax.ppermute(value, axis, [(i, (i + stride) % count) for i in range(count)])


def gather_blocks(block, last_by_ring):
    depth, y, core = factors(lax.axis_size("seq"))
    own, other = [block], []
    for k in range(depth):
        last = k == depth - 1
        if y == 2:
            if last and last_by_ring and depth > 1:
                other.append(ring(other[-1], "seq", core * y))
            else:
                other.append(swap(own[k], "seq", core, y))
        if not last:
            own.append(ring(own[k], "seq", core * y))
    return [[own[k]] + ([other[k]] if y == 2 else []) for k in range(depth)]


def rms_scale(values32, gain):
    return (
        values32 * lax.rsqrt(jnp.mean(values32 * values32, axis=-1, keepdims=True) + 1e-06) * gain
    )


def feed_partial(tokens, enc_gain, first_weight, second_weight):
    enc_norm = rms_scale(tokens.astype(jnp.float32), enc_gain).astype(jnp.bfloat16)
    inner = jax.nn.relu(jnp.dot(enc_norm, first_weight, preferred_element_type=jnp.float32)).astype(
        jnp.bfloat16
    )
    return jnp.dot(inner, second_weight, preferred_element_type=jnp.float32).astype(jnp.bfloat16)


def tp_sum(value):
    if lax.axis_size("tp") == 2:
        return value.astype(jnp.float32) + swap(value, "tp", 1, 2).astype(jnp.float32)
    return lax.psum(value, "tp").astype(jnp.float32)


def ordered(flag, first, second, axis):
    return jnp.concatenate(
        [jnp.where(flag, first, second), jnp.where(flag, second, first)], axis=axis
    )


def attend_kernel(heads, spans, q_ref, k_ref, v_ref, o_ref):
    for h in range(heads):
        cols = slice(h * HD, (h + 1) * HD)
        for s in range(spans):
            rows = slice(s * M, (s + 1) * M)
            keys = slice(s * KEYS, (s + 1) * KEYS)
            scores = lax.dot_general(
                q_ref[rows, cols],
                k_ref[keys, cols],
                (((1,), (1,)), ((), ())),
                preferred_element_type=jnp.float32,
            ) * HD ** (-0.5)
            shifted = jnp.exp(scores - jnp.max(scores, axis=-1, keepdims=True))
            probs = (shifted / jnp.sum(shifted, axis=-1, keepdims=True)).astype(jnp.bfloat16)
            o_ref[rows, cols] = jnp.dot(
                probs, v_ref[keys, cols], preferred_element_type=jnp.float32
            ).astype(jnp.bfloat16)


def attend(query, keys, values):
    rows, width = query.shape
    spans = rows // M
    heads = 2 if (width // HD) % 2 == 0 else 1
    block = heads * HD
    return pl.pallas_call(
        functools.partial(attend_kernel, heads, spans),
        grid=(width // block,),
        in_specs=[
            pl.BlockSpec((rows, block), lambda i: (0, i)),
            pl.BlockSpec((spans * KEYS, block), lambda i: (0, i)),
            pl.BlockSpec((spans * KEYS, block), lambda i: (0, i)),
        ],
        out_specs=pl.BlockSpec((rows, block), lambda i: (0, i)),
        out_shape=jax.ShapeDtypeStruct((rows, width), jnp.bfloat16),
        compiler_params=pltpu.CompilerParams(vmem_limit_bytes=24 * 1024 * 1024),
        cost_estimate=pl.CostEstimate(
            flops=4 * rows * KEYS * width,
            bytes_accessed=4 * (rows + spans * KEYS) * width,
            transcendentals=rows * KEYS * width // HD,
        ),
        name="attend",
    )(query, keys, values)


def per_device(
    hidden,
    neighbours,
    enc_gain,
    enc_w1,
    enc_w2,
    key_weight,
    value_weight,
    dec_gain,
    query_weight,
    out_weight,
):
    tok_rows, feat = hidden.shape
    span_count, key_rows, width = neighbours.shape
    n_seq, n_tp = lax.axis_size("seq"), lax.axis_size("tp")
    depth, n_y, n_core = factors(n_seq)
    me = lax.axis_index("seq")
    tp_at = lax.axis_index("tp")
    core_at, y_at, z_at = me % n_core, (me // n_core) % n_y, me // (n_core * n_y)
    core_first, y_first = core_at == 0, y_at == 0

    q_rows, q_cols = query_weight.shape
    per_core = q_cols // n_core
    streams = 2
    q_width = per_core // streams
    q_blocks = []
    for h in range(streams):
        mine = lax.dynamic_slice(query_weight, (0, core_at * per_core + h * q_width), (q_rows, q_width))
        if n_core == 2:
            theirs = lax.dynamic_slice(
                query_weight, (0, (1 - core_at) * per_core + h * q_width), (q_rows, q_width)
            )
            mine = ordered(core_first, mine, swap(theirs, "seq", 1, 2), 0)
        q_blocks.append(gather_blocks(mine, h == 0))

    if n_tp == 2:
        features = ordered(tp_at == 0, hidden, swap(hidden, "tp", 1, 2), 1)
    else:
        features = lax.all_gather(hidden, "tp", axis=1, tiled=True)
    dec_norm = rms_scale(features.astype(jnp.float32), dec_gain).astype(jnp.bfloat16)
    if n_core == 2:
        dec_norm = jnp.concatenate([dec_norm, swap(dec_norm, "seq", 1, 2)], axis=0)

    flat = neighbours.reshape(span_count * key_rows, width)
    pieces = 2
    piece_rows = flat.shape[0] // pieces
    encoded = []
    for i in range(pieces):
        part = flat[i * piece_rows : (i + 1) * piece_rows]
        summed = tp_sum(feed_partial(part, enc_gain, enc_w1, enc_w2))
        encoded.append((part.astype(jnp.float32) + summed).astype(jnp.bfloat16))
    earlier = lax.ppermute(
        encoded[-1][piece_rows - key_rows :], "seq", [(i, i + 1) for i in range(n_seq - 1)]
    )
    encoded = jnp.concatenate([earlier] + encoded, axis=0)
    keys = jnp.dot(encoded, key_weight, preferred_element_type=jnp.float32).astype(jnp.bfloat16)
    values = jnp.dot(encoded, value_weight, preferred_element_type=jnp.float32).astype(jnp.bfloat16)

    group = q_rows * n_core
    parts = []
    for h in range(streams):
        total = jnp.zeros((dec_norm.shape[0], q_width), jnp.float32)
        for k in range(depth):
            for j in range(n_y):
                at = ((z_at - k) % depth) * n_y + (y_at + j) % n_y
                total = total + jnp.dot(
                    lax.dynamic_slice(dec_norm, (0, at * group), (dec_norm.shape[0], group)),
                    q_blocks[h][k][j],
                    preferred_element_type=jnp.float32,
                )
        parts.append(total.astype(jnp.bfloat16))
    query = jnp.concatenate(parts, axis=1)
    if n_core == 2:
        query = ordered(core_first, query[:tok_rows], swap(query[tok_rows:], "seq", 1, 2), 1)

    grouped = jnp.pad(query, ((1, M - 1), (0, 0)))
    attn = attend(grouped, keys, values)[1 : tok_rows + 1]
    position = me * tok_rows + jnp.arange(tok_rows, dtype=jnp.int32)[:, None]
    attn = jnp.where(position >= M - 1, attn, jnp.zeros_like(attn))
    if n_core == 2:
        attn = jnp.concatenate([attn, swap(attn, "seq", 1, 2)], axis=0)

    o_rows, o_cols = out_weight.shape
    half = o_rows // streams
    o_blocks = [
        gather_blocks(out_weight[h * half : (h + 1) * half], h == 0) for h in range(streams)
    ]
    products = []
    for k in range(depth):
        made = []
        for j in range(n_y):
            total = sum(
                jnp.dot(
                    attn[:, h * half : (h + 1) * half],
                    o_blocks[h][k][j],
                    preferred_element_type=jnp.float32,
                )
                for h in range(streams)
            )
            made.append(total.astype(jnp.bfloat16))
        if n_core == 2:
            here = [m[:tok_rows] for m in made]
            there = swap(jnp.concatenate([m[tok_rows:] for m in made], axis=1), "seq", 1, 2)
            there = [there[:, j * o_cols : (j + 1) * o_cols] for j in range(n_y)]
            made = [ordered(core_first, a, b, 1) for a, b in zip(here, there)]
        products.append(ordered(y_first, made[0], made[1], 1) if n_y == 2 else made[0])

    if n_tp == 2 and depth % 4 == 0:
        pairs = depth // 2
        kept = []
        for p in range(pairs):
            mine = ((z_at - p) % depth) // pairs == tp_at
            sent = jnp.where(mine, products[p + pairs], products[p])
            stay = jnp.where(mine, products[p], products[p + pairs])
            kept.append(stay.astype(jnp.float32) + swap(sent, "tp", 1, 2).astype(jnp.float32))
        stacked = jnp.stack(kept, axis=0)
        order = (z_at - jnp.arange(pairs)) % pairs
        branch = jnp.take(stacked, order, axis=0)
        branch = jnp.moveaxis(branch, 0, 1).reshape(tok_rows, feat)
    else:
        stacked = jnp.stack(products, axis=0)
        order = (z_at - jnp.arange(depth)) % depth
        whole = jnp.moveaxis(jnp.take(stacked, order, axis=0), 0, 1).reshape(tok_rows, feat * n_tp)
        branch = lax.psum_scatter(whole, "tp", scatter_dimension=1, tiled=True).astype(jnp.float32)
    return (hidden.astype(jnp.float32) + branch).astype(jnp.bfloat16)


def solution(mesh):
    placed = (
        P("seq", "tp"),
        P("seq", None, None),
        P(),
        P(None, "tp"),
        P("tp", None),
        P(None, "tp"),
        P(None, "tp"),
        P(),
        P("seq", "tp"),
        P("tp", "seq"),
    )
    return jax.shard_map(
        per_device, mesh=mesh, in_specs=placed, out_specs=P("seq", "tp"), check_vma=False
    )
```

time: 429 us -> 337 us (0.79)
  waiting for transfers between devices: 315 us -> 172 us
  starting transfers between devices: 3.46 us -> 57.4 us
  Pallas kernels: 0 us -> 28.5 us
  matrix products: 65.6 us -> 47.6 us
  between operations: 13.3 us -> 0.81 us
  local copies, waits for them, and re-layouts: 15.9 us -> 10.6 us
  other arithmetic: 15.1 us -> 19.5 us
    all_gather x3 -> x0, waiting for transfers between devices: 216 us -> none  [the longest x1 107 us: per_device(): lax.all_gather(query_weight, 'seq', axis=0, tiled=True)]
    ppermute x1 -> x43, waiting for transfers between devices: 0.93 us -> 172 us  [the longest x28 93.6 us: swap(): return lax.ppermute(value, axis, pairs)]
    psum x1 -> x0, waiting for transfers between devices: 67.5 us -> none  [encode(): lax.psum(feed_partial(flat, enc_gain, enc_w1, enc_w2).astype(jnp.bfloat16...]
    ppermute x1 -> x43, starting transfers between devices: 3.12 us -> 57.4 us  [the longest x28 28.5 us: swap(): return lax.ppermute(value, axis, pairs)]
    reduce_scatter x1 -> x0, waiting for transfers between devices: 30.1 us -> none  [per_device(): lax.psum_scatter(partial_value.astype(jnp.bfloat16), 'tp', scatter_dimens...]
    pallas_call x0 -> x1, Pallas kernels: none -> 28.5 us  [attend(): pl.pallas_call(functools.partial(attend_kernel, heads, spans), grid=(widt...]
    dot_general x7 -> x36, matrix products: 65.6 us -> 47.6 us  [the longest x2 14.2 us: feed_partial(): jnp.dot(inner, second_weight, preferred_element_type=jnp.float32)]
    unnamed x23 -> x32, local copies, waits for them, and re-layouts: 13 us -> 2.51 us
  transfers between devices with their start and end apart: 6 -> 43, of which waited for: 6 -> 19; matrix products, arithmetic and copies ran while one was open for 18% -> 19% of each run, Pallas kernels for 0% -> 0%
where the time goes in v1:
time: 337 us; the launch traced here: 336 us
  waiting for transfers between devices  172 us (51%)
  starting transfers between devices  57.4 us (17%)
  matrix products  47.6 us (14%)
  Pallas kernels  28.5 us (8%)
  other arithmetic  19.5 us (6%)
  local copies, waits for them, and re-layouts  10.6 us (3%)
    ppermute x28, waiting for transfers between devices, swap(): return lax.ppermute(value, axis, pairs)  93.6 us
    ppermute x14, waiting for transfers between devices, ring(): lax.ppermute(value, axis, [(i, (i + stride) % count) for i in range(count)])  77.9 us
    ppermute x28, starting transfers between devices, swap(): return lax.ppermute(value, axis, pairs)  28.5 us
    pallas_call x1, Pallas kernels, attend(): pl.pallas_call(functools.partial(attend_kernel, heads, spans), grid=(widt...  28.5 us
    ppermute x14, starting transfers between devices, ring(): lax.ppermute(value, axis, [(i, (i + stride) % count) for i in range(count)])  27.6 us
    dot_general x2, matrix products, feed_partial(): jnp.dot(inner, second_weight, preferred_element_type=jnp.float32)  14.2 us
    dot_general x16, matrix products, per_device(): jnp.dot(attn[:, h * half:(h + 1) * half], o_blocks[h][k][j], preferred_el...  11.9 us
    dot_general x1, matrix products, per_device(): jnp.dot(encoded, key_weight, preferred_element_type=jnp.float32)  7.23 us
  transfers between devices with their start and end apart: 43, of which 19 were waited for; matrix products, arithmetic and copies ran while one was open for 19% of the time, Pallas kernels for 0%

profile of v1, /device:TPU:0, one launch (start us, length us, event | category | flops | bytes accessed | tf_op | source)
XLA Modules:
  0.0 336.0 jit_solution(4490879235934927134)
XLA Ops:
  0.0 2.9 collective-permute-start
  2.9 1.8 constant_dynamic-slice_fusion.1
  4.8 1.9 fusion.6
  6.7 1.7 fusion.8
  8.4 7.1 %convolution_convert_fusion.3 = bf16[512,896]{1,0:T(8,128)(2,1)} fusion(bf16[1792,896]{1,0:T(8,128)(2,1)S(1)} %copy-done, bf16[512,896]{1,0:T(8,128)(2,1)} %get-tuple-element.16, bf16[896,1792]{1,0:T(8,128)(2,1)} %param.13), kind=kOutput, calls=%fused_computation.52 | convolution fusion | flops 3290628096 | bytes 8257536 | tf_op jit(solution)/shard_map/dot_general | solution.py:60
  15.6 7.1 %convolution_convert_fusion.2 = bf16[512,896]{1,0:T(8,128)(2,1)} fusion(bf16[1792,896]{1,0:T(8,128)(2,1)S(1)} %copy-done, bf16[512,896]{1,0:T(8,128)(2,1)} %get-tuple-element.15, bf16[896,1792]{1,0:T(8,128)(2,1)} %param.13), kind=kOutput, calls=%fused_computation.51 | convolution fusion | flops 3290628096 | bytes 8257536 | tf_op jit(solution)/shard_map/dot_general | solution.py:60
  22.7 2.0 collective-permute-start.21
  24.7 2.6 collective-permute-done
  27.2 1.7 broadcast_select_fusion.2
  31.1 2.2 collective-permute-start.4
  33.3 13.6 %collective-permute-done.19 = bf16[512,896]{1,0:T(8,128)(2,1)} collective-permute-done((bf16[512,896]{1,0:T(8,128)(2,1)}, bf16[512,896]{1,0:T(8,128)(2,1)}, u32[]{:S(2)}, u32[]{:S(2)}) %collective-permute-start.19) | collective-permute-done | bytes 917536 | tf_op jit(solution)/shard_map/ppermute | solution.py:26
  46.9 18.8 %collective-permute-done.21 = bf16[512,896]{1,0:T(8,128)(2,1)} collective-permute-done((bf16[512,896]{1,0:T(8,128)(2,1)}, bf16[512,896]{1,0:T(8,128)(2,1)}, u32[]{:S(2)}, u32[]{:S(2)}) %collective-permute-start.21) | collective-permute-done | bytes 917536 | tf_op jit(solution)/shard_map/ppermute | solution.py:26
  65.8 2.3 fusion.9
  68.1 1.3 collective-permute-start.20
  69.5 2.4 collective-permute-start.3
  72.2 2.1 collective-permute-start.12
  74.2 8.3 %collective-permute-start.6 = (bf16[512,512]{1,0:T(8,128)(2,1)S(1)}, bf16[512,512]{1,0:T(8,128)(2,1)S(1)}, u32[]{:S(2)}, u32[]{:S(2)}) collective-permute-start(bf16[512,512]{1,0:T(8,128)(2,1)S(1)} %collective-permute-done.4), channel_id=1, source_target_pairs={{0,8},{2,10},{4,12},{6,14},{8,16},{10,18},{12,20},{14,22},{16,24},... | collective-permute-start | bytes 1572872 | tf_op jit(solution)/shard_map/ppermute | solution.py:31
  82.5 7.2 %convolution_convert_fusion.v_ref = bf16[1280,2048]{1,0:T(8,128)(2,1)S(1)} fusion(bf16[896,2048]{1,0:T(8,128)(2,1)S(1)} %copy-done.13, bf16[512,896]{1,0:T(8,128)(2,1)S(1)} %get-tuple-element.18, bf16[512,896]{1,0:T(8,128)(2,1)S(1)} %get-tuple-element.17, bf16[256,896]{1,0:T(8,128)(2,1)S(1)} %collective-permute-done.20), kind=kOutput, calls=%fused_computation.17 | convolution fusion | flops 4707123200 | bytes 11206656 | tf_op jit(solution)/shard_map/dot_general | solution.py:175
  89.8 3.0 collective-permute-start.5
  92.8 1.6 collective-permute-start.14
  95.7 4.3 %collective-permute-done.6 = bf16[512,512]{1,0:T(8,128)(2,1)S(1)} collective-permute-done((bf16[512,512]{1,0:T(8,128)(2,1)S(1)}, bf16[512,512]{1,0:T(8,128)(2,1)S(1)}, u32[]{:S(2)}, u32[]{:S(2)}) %collective-permute-start.6) | collective-permute-done | bytes 524320 | tf_op jit(solution)/shard_map/ppermute | solution.py:31
  100.6 1.8 collective-permute-start.7
  102.4 8.8 %collective-permute-done.14 = bf16[512,512]{1,0:T(8,128)(2,1)S(1)} collective-permute-done((bf16[512,512]{1,0:T(8,128)(2,1)S(1)}, bf16[512,512]{1,0:T(8,128)(2,1)S(1)}, u32[]{:S(2)}, u32[]{:S(2)}) %collective-permute-start.14) | collective-permute-done | bytes 524320 | tf_op jit(solution)/shard_map/ppermute | solution.py:31
  113.7 1.8 collective-permute-start.15
  115.5 13.6 %collective-permute-done.7 = bf16[512,512]{1,0:T(8,128)(2,1)S(1)} collective-permute-done((bf16[512,512]{1,0:T(8,128)(2,1)S(1)}, bf16[512,512]{1,0:T(8,128)(2,1)S(1)}, u32[]{:S(2)}, u32[]{:S(2)}) %collective-permute-start.7) | collective-permute-done | bytes 524320 | tf_op jit(solution)/shard_map/ppermute | solution.py:26
  129.1 7.2 %collective-permute-start.9 = (bf16[512,512]{1,0:T(8,128)(2,1)S(1)}, bf16[512,512]{1,0:T(8,128)(2,1)S(1)}, u32[]{:S(2)}, u32[]{:S(2)}) collective-permute-start(bf16[512,512]{1,0:T(8,128)(2,1)S(1)} %collective-permute-done.7), channel_id=1, source_target_pairs={{0,8},{2,10},{4,12},{6,14},{8,16},{10,18},{12,20},{14,22},{16,24},... | collective-permute-start | bytes 1572872 | tf_op jit(solution)/shard_map/ppermute | solution.py:31
  138.6 10.1 %collective-permute-done.9 = bf16[512,512]{1,0:T(8,128)(2,1)S(1)} collective-permute-done((bf16[512,512]{1,0:T(8,128)(2,1)S(1)}, bf16[512,512]{1,0:T(8,128)(2,1)S(1)}, u32[]{:S(2)}, u32[]{:S(2)}) %collective-permute-start.9) | collective-permute-done | bytes 524320 | tf_op jit(solution)/shard_map/ppermute | solution.py:31
  149.6 2.0 collective-permute-done.17
  152.1 4.5 %collective-permute-start.18 = (bf16[256,1024]{1,0:T(8,128)(2,1)S(1)}, bf16[256,1024]{1,0:T(8,128)(2,1)S(1)}, u32[]{:S(2)}, u32[]{:S(2)}) collective-permute-start(bf16[256,1024]{1,0:T(8,128)(2,1)S(1)} %pad_maximum_fusion.6), channel_id=1, source_target_pairs={{0,2},{2,0},{4,6},{6,4},{8,10},{10,8},{12,14},{14,12},{16,18},{18,... | collective-permute-start | bytes 1572872 | tf_op jit(solution)/shard_map/ppermute | solution.py:26
  156.5 7.2 %convolution_convert_fusion.1.k_ref = bf16[1280,2048]{1,0:T(8,128)(2,1)S(1)} fusion(bf16[896,2048]{1,0:T(8,128)(2,1)S(1)} %copy-done.14, bf16[512,896]{1,0:T(8,128)(2,1)S(1)} %get-tuple-element.18, bf16[512,896]{1,0:T(8,128)(2,1)S(1)} %get-tuple-element.17, bf16[256,896]{1,0:T(8,128)(2,1)S(1)} %collective-permute-done.20), kind=kOutput, calls=%fused_computation.18 | convolution fusion | flops 4707123200 | bytes 11206656 | tf_op jit(solution)/shard_map/dot_general | solution.py:174
  164.3 28.5 %attend.1 = bf16[320,2048]{1,0:T(8,128)(2,1)S(1)} custom-call(bf16[320,2048]{1,0:T(8,128)(2,1)S(1)} %fusion.20.q_ref, bf16[1280,2048]{1,0:T(8,128)(2,1)S(1)} %convolution_convert_fusion.1.k_ref, bf16[1280,2048]{1,0:T(8,128)(2,1)S(1)} %convolution_convert_fusion.v_ref), custom_call_target="tpu_custom_call" | custom-call | flops 671088640 | bytes 13107200 | tf_op jit(solution)/shard_map/attend/pallas_call | solution.py:99
  193.2 0.7 copy-done.5
  194.0 1.0 fusion.59
  195.0 3.0 collective-permute-start.28
  198.0 1.6 collective-permute-start.26
  199.5 0.8 collective-permute-start.24
  200.4 1.2 collective-permute-start.23
  201.6 11.5 %collective-permute-done.28 = bf16[1024,256]{1,0:T(8,128)(2,1)} collective-permute-done((bf16[1024,256]{1,0:T(8,128)(2,1)}, bf16[1024,256]{1,0:T(8,128)(2,1)}, u32[]{:S(2)}, u32[]{:S(2)}) %collective-permute-start.28) | collective-permute-done | bytes 524320 | tf_op jit(solution)/shard_map/ppermute | solution.py:31
  213.1 11.2 %collective-permute-done.26 = bf16[1024,256]{1,0:T(8,128)(2,1)} collective-permute-done((bf16[1024,256]{1,0:T(8,128)(2,1)}, bf16[1024,256]{1,0:T(8,128)(2,1)}, u32[]{:S(2)}, u32[]{:S(2)}) %collective-permute-start.26) | collective-permute-done | bytes 524320 | tf_op jit(solution)/shard_map/ppermute | solution.py:31
  224.3 1.0 collective-permute-start.35
  225.3 1.0 copy-done.8
  226.4 1.7 fusion.31
  229.0 6.4 %collective-permute-done.29 = bf16[1024,256]{1,0:T(8,128)(2,1)S(1)} collective-permute-done((bf16[1024,256]{1,0:T(8,128)(2,1)}, bf16[1024,256]{1,0:T(8,128)(2,1)S(1)}, u32[]{:S(2)}, u32[]{:S(2)}) %collective-permute-start.29) | collective-permute-done | bytes 524320 | tf_op jit(solution)/shard_map/ppermute | solution.py:31
  235.4 1.0 collective-permute-start.34
  236.9 9.4 %collective-permute-done.27 = bf16[1024,256]{1,0:T(8,128)(2,1)S(1)} collective-permute-done((bf16[1024,256]{1,0:T(8,128)(2,1)}, bf16[1024,256]{1,0:T(8,128)(2,1)S(1)}, u32[]{:S(2)}, u32[]{:S(2)}) %collective-permute-start.27) | collective-permute-done | bytes 524320 | tf_op jit(solution)/shard_map/ppermute | solution.py:31
  247.4 1.6 collective-permute-start.30
  249.0 1.5 fusion.68
  250.5 10.7 %collective-permute-done.31 = bf16[1024,256]{1,0:T(8,128)(2,1)S(1)} collective-permute-done((bf16[1024,256]{1,0:T(8,128)(2,1)S(1)}, bf16[1024,256]{1,0:T(8,128)(2,1)S(1)}, u32[]{:S(2)}, u32[]{:S(2)}) %collective-permute-start.31) | collective-permute-done | bytes 524320 | tf_op jit(solution)/shard_map/ppermute | solution.py:26
  261.7 9.9 %collective-permute-done.30 = bf16[1024,256]{1,0:T(8,128)(2,1)S(1)} collective-permute-done((bf16[1024,256]{1,0:T(8,128)(2,1)S(1)}, bf16[1024,256]{1,0:T(8,128)(2,1)S(1)}, u32[]{:S(2)}, u32[]{:S(2)}) %collective-permute-start.30) | collective-permute-done | bytes 524320 | tf_op jit(solution)/shard_map/ppermute | solution.py:26
  272.0 1.3 collective-permute-start.39
  273.4 1.8 collective-permute-done.38
  275.2 1.5 fusion.24
  276.9 1.5 fusion.71
  279.0 1.5 fusion.27
  282.1 6.1 %collective-permute-done.37 = bf16[1024,256]{1,0:T(8,128)(2,1)S(1)} collective-permute-done((bf16[1024,256]{1,0:T(8,128)(2,1)S(1)}, bf16[1024,256]{1,0:T(8,128)(2,1)S(1)}, u32[]{:S(2)}, u32[]{:S(2)}) %collective-permute-start.37) | collective-permute-done | bytes 524320 | tf_op jit(solution)/shard_map/ppermute | solution.py:31
  289.2 8.4 %collective-permute-done.39 = bf16[1024,256]{1,0:T(8,128)(2,1)S(1)} collective-permute-done((bf16[1024,256]{1,0:T(8,128)(2,1)S(1)}, bf16[1024,256]{1,0:T(8,128)(2,1)S(1)}, u32[]{:S(2)}, u32[]{:S(2)}) %collective-permute-start.39) | collective-permute-done | bytes 524320 | tf_op jit(solution)/shard_map/ppermute | solution.py:31
  298.7 1.6 collective-permute-start.33
  300.7 1.0 collective-permute-start.42
  301.7 11.7 %collective-permute-done.33 = bf16[256,1024]{0,1:T(8,128)(2,1)S(1)} collective-permute-done((bf16[256,1024]{0,1:T(8,128)(2,1)S(1)}, bf16[256,1024]{0,1:T(8,128)(2,1)S(1)}, u32[]{:S(2)}, u32[]{:S(2)}) %collective-permute-start.33) | collective-permute-done | bytes 524320 | tf_op jit(solution)/shard_map/ppermute | solution.py:26
  313.6 10.7 %collective-permute-done.42 = bf16[256,1024]{0,1:T(8,128)(2,1)S(1)} collective-permute-done((bf16[256,1024]{0,1:T(8,128)(2,1)S(1)}, bf16[256,1024]{0,1:T(8,128)(2,1)S(1)}, u32[]{:S(2)}, u32[]{:S(2)}) %collective-permute-start.42) | collective-permute-done | bytes 524320 | tf_op jit(solution)/shard_map/ppermute | solution.py:26
  324.6 2.0 gather_fusion
  326.7 3.2 broadcast_select_fusion
  329.8 3.1 copy.27
  332.9 3.1 add_convert_fusion
  (144 shorter events, 19.9 us)
Async XLA Ops:
  0.0 8.4 %copy-start = (bf16[1792,896]{1,0:T(8,128)(2,1)S(1)}, bf16[1792,896]{1,0:T(8,128)(2,1)}, u32[]{:S(2)}) copy-start(bf16[1792,896]{1,0:T(8,128)(2,1)} %param.14) | copy-start | bytes 9633796
  0.0 6.7 %copy-start.12 = (f32[896]{0:T(1024)S(1)}, f32[896]{0:T(1024)}, u32[]{:S(2)}) copy-start(f32[896]{0:T(1024)} %param.12) | copy-start | bytes 10756
  0.0 27.2 %collective-permute-start = (bf16[256,2048]{1,0:T(8,128)(2,1)}, bf16[256,2048]{1,0:T(8,128)(2,1)}, u32[]{:S(2)}, u32[]{:S(2)}) collective-permute-start(bf16[256,2048]{1,0:T(8,128)(2,1)} %param.10), channel_id=1, source_target_pairs={{0,1},{1,0},{2,3},{3,2},{4,5},{5,4},{6,7},{7,6},{8,9},{9,8},{10,11... | collective-permute-start | bytes 3145736 | tf_op jit(solution)/shard_map/ppermute | solution.py:26
  2.9 3.8 %copy-start.2 = (bf16[4,256,896]{2,1,0:T(8,128)(2,1)S(1)}, bf16[4,256,896]{2,1,0:T(8,128)(2,1)}, u32[]{:S(2)}) copy-start(bf16[4,256,896]{2,1,0:T(8,128)(2,1)} %param.11) | copy-start | bytes 5505028
  4.8 25.6 %collective-permute-start.2 = (bf16[256,512]{1,0:T(8,128)(2,1)}, bf16[256,512]{1,0:T(8,128)(2,1)S(1)}, u32[]{:S(2)}, u32[]{:S(2)}) collective-permute-start(bf16[256,512]{1,0:T(8,128)(2,1)} %constant_dynamic-slice_fusion.1), channel_id=1, source_target_pairs={{0,2},{2,0},{4,6},{6,4},{8,10},{10,8},{12,14},{14,12},{16,18},{18,... | collective-permute-start | bytes 786440 | tf_op jit(solution)/shard_map/ppermute | solution.py:26
  15.5 31.4 %collective-permute-start.19 = (bf16[512,896]{1,0:T(8,128)(2,1)}, bf16[512,896]{1,0:T(8,128)(2,1)}, u32[]{:S(2)}, u32[]{:S(2)}) collective-permute-start(bf16[512,896]{1,0:T(8,128)(2,1)} %convolution_convert_fusion.3), channel_id=1, source_target_pairs={{0,1},{1,0},{2,3},{3,2},{4,5},{5,4},{6,7},{7,6},{8,9},{9,8},{10,11... | collective-permute-start | bytes 2752520 | tf_op jit(solution)/shard_map/ppermute | solution.py:26
  22.7 43.0 %collective-permute-start.21 = (bf16[512,896]{1,0:T(8,128)(2,1)}, bf16[512,896]{1,0:T(8,128)(2,1)}, u32[]{:S(2)}, u32[]{:S(2)}) collective-permute-start(bf16[512,896]{1,0:T(8,128)(2,1)} %convolution_convert_fusion.2), channel_id=1, source_target_pairs={{0,1},{1,0},{2,3},{3,2},{4,5},{5,4},{6,7},{7,6},{8,9},{9,8},{10,11... | collective-permute-start | bytes 2752520 | tf_op jit(solution)/shard_map/ppermute | solution.py:26
  28.9 0.7 copy-start.11
  29.6 1.2 copy-start.7
  29.7 36.1 %copy-start.9 = (bf16[512,896]{1,0:T(8,128)(2,1)S(1)}, bf16[512,896]{1,0:T(8,128)(2,1)}, u32[]{:S(2)}) copy-start(bf16[512,896]{1,0:T(8,128)(2,1)} %convolution_convert_fusion.3) | copy-start | bytes 2752516
  29.7 36.1 %copy-start.10 = (bf16[512,896]{1,0:T(8,128)(2,1)S(1)}, bf16[512,896]{1,0:T(8,128)(2,1)}, u32[]{:S(2)}) copy-start(bf16[512,896]{1,0:T(8,128)(2,1)} %convolution_convert_fusion.2) | copy-start | bytes 2752516
  30.3 35.5 %copy-start.3 = (bf16[4,256,896]{2,1,0:T(8,128)(2,1)S(1)}, bf16[4,256,896]{2,1,0:T(8,128)(2,1)}, u32[]{:S(2)}) copy-start(bf16[4,256,896]{2,1,0:T(8,128)(2,1)} %param.11) | copy-start | bytes 5505028
  30.3 62.5 %collective-permute-start.1 = (bf16[256,4096]{1,0:T(8,128)(2,1)S(1)}, bf16[256,4096]{1,0:T(8,128)(2,1)S(1)}, u32[]{:S(2)}, u32[]{:S(2)}) collective-permute-start(bf16[256,4096]{1,0:T(8,128)(2,1)S(1)} %fusion.2), channel_id=1, source_target_pairs={{0,2},{2,0},{4,6},{6,4},{8,10},{10,8},{12,14},{14,12},{16,18},{18,... | collective-permute-start | bytes 6291464 | tf_op jit(solution)/shard_map/ppermute | solution.py:26
  31.1 41.1 %collective-permute-start.4 = (bf16[512,512]{1,0:T(8,128)(2,1)S(1)}, bf16[512,512]{1,0:T(8,128)(2,1)S(1)}, u32[]{:S(2)}, u32[]{:S(2)}) collective-permute-start(bf16[512,512]{1,0:T(8,128)(2,1)S(1)} %pad_maximum_fusion.7), channel_id=1, source_target_pairs={{0,8},{2,10},{4,12},{6,14},{8,16},{10,18},{12,20},{14,22},{16,24},... | collective-permute-start | bytes 1572872 | tf_op jit(solution)/shard_map/ppermute | solution.py:31
  33.3 38.6 %collective-permute-start.10 = (bf16[256,512]{1,0:T(8,128)(2,1)S(1)}, bf16[256,512]{1,0:T(8,128)(2,1)S(1)}, u32[]{:S(2)}, u32[]{:S(2)}) collective-permute-start(bf16[256,512]{1,0:T(8,128)(2,1)S(1)} %get-tuple-element.27), channel_id=1, source_target_pairs={{0,2},{2,0},{4,6},{6,4},{8,10},{10,8},{12,14},{14,12},{16,18},{18,... | collective-permute-start | bytes 786440 | tf_op jit(solution)/shard_map/ppermute | solution.py:26
  65.8 16.8 %copy-start.13 = (bf16[896,2048]{1,0:T(8,128)(2,1)S(1)}, bf16[896,2048]{1,0:T(8,128)(2,1)}, u32[]{:S(2)}) copy-start(bf16[896,2048]{1,0:T(8,128)(2,1)} %param.16) | copy-start | bytes 11010052
  68.1 6.1 %collective-permute-start.20 = (bf16[256,896]{1,0:T(8,128)(2,1)S(1)}, bf16[256,896]{1,0:T(8,128)(2,1)S(1)}, u32[]{:S(2)}, u32[]{:S(2)}) collective-permute-start(bf16[256,896]{1,0:T(8,128)(2,1)S(1)} %slice.156), channel_id=1, source_target_pairs={{0,2},{2,4},{4,6},{6,8},{8,10},{10,12},{12,14},{14,16},{16,18},{18... | collective-permute-start | bytes 1376264 | tf_op jit(solution)/shard_map/ppermute | solution.py:170
  69.5 26.1 %collective-permute-start.3 = (bf16[512,512]{1,0:T(8,128)(2,1)S(1)}, bf16[512,512]{1,0:T(8,128)(2,1)S(1)}, u32[]{:S(2)}, u32[]{:S(2)}) collective-permute-start(bf16[512,512]{1,0:T(8,128)(2,1)S(1)} %pad_maximum_fusion.7), channel_id=1, source_target_pairs={{0,4},{2,6},{4,0},{6,2},{8,12},{10,14},{12,8},{14,10},{16,20},{18,... | collective-permute-start | bytes 1572872 | tf_op jit(solution)/shard_map/ppermute | solution.py:26
  72.1 28.5 %collective-permute-start.11 = (bf16[512,512]{1,0:T(8,128)(2,1)S(1)}, bf16[512,512]{1,0:T(8,128)(2,1)S(1)}, u32[]{:S(2)}, u32[]{:S(2)}) collective-permute-start(bf16[512,512]{1,0:T(8,128)(2,1)S(1)} %pad_maximum_fusion.8), channel_id=1, source_target_pairs={{0,4},{2,6},{4,0},{6,2},{8,12},{10,14},{12,8},{14,10},{16,20},{18,... | collective-permute-start | bytes 1572872 | tf_op jit(solution)/shard_map/ppermute | solution.py:26
  72.2 17.6 %collective-permute-start.12 = (bf16[512,512]{1,0:T(8,128)(2,1)S(1)}, bf16[512,512]{1,0:T(8,128)(2,1)S(1)}, u32[]{:S(2)}, u32[]{:S(2)}) collective-permute-start(bf16[512,512]{1,0:T(8,128)(2,1)S(1)} %pad_maximum_fusion.8), channel_id=1, source_target_pairs={{0,8},{2,10},{4,12},{6,14},{8,16},{10,18},{12,20},{14,22},{16,24},... | collective-permute-start | bytes 1572872 | tf_op jit(solution)/shard_map/ppermute | solution.py:31
  74.2 25.7 %collective-permute-start.6 = (bf16[512,512]{1,0:T(8,128)(2,1)S(1)}, bf16[512,512]{1,0:T(8,128)(2,1)S(1)}, u32[]{:S(2)}, u32[]{:S(2)}) collective-permute-start(bf16[512,512]{1,0:T(8,128)(2,1)S(1)} %collective-permute-done.4), channel_id=1, source_target_pairs={{0,8},{2,10},{4,12},{6,14},{8,16},{10,18},{12,20},{14,22},{16,24},... | collective-permute-start | bytes 1572872 | tf_op jit(solution)/shard_map/ppermute | solution.py:31
  89.8 23.9 %collective-permute-start.5 = (bf16[512,512]{1,0:T(8,128)(2,1)S(1)}, bf16[512,512]{1,0:T(8,128)(2,1)S(1)}, u32[]{:S(2)}, u32[]{:S(2)}) collective-permute-start(bf16[512,512]{1,0:T(8,128)(2,1)S(1)} %collective-permute-done.4), channel_id=1, source_target_pairs={{0,4},{2,6},{4,0},{6,2},{8,12},{10,14},{12,8},{14,10},{16,20},{18,... | collective-permute-start | bytes 1572872 | tf_op jit(solution)/shard_map/ppermute | solution.py:26
  92.8 18.4 %collective-permute-start.14 = (bf16[512,512]{1,0:T(8,128)(2,1)S(1)}, bf16[512,512]{1,0:T(8,128)(2,1)S(1)}, u32[]{:S(2)}, u32[]{:S(2)}) collective-permute-start(bf16[512,512]{1,0:T(8,128)(2,1)S(1)} %collective-permute-done.12), channel_id=1, source_target_pairs={{0,8},{2,10},{4,12},{6,14},{8,16},{10,18},{12,20},{14,22},{16,24},... | collective-permute-start | bytes 1572872 | tf_op jit(solution)/shard_map/ppermute | solution.py:31
  95.6 42.1 %collective-permute-start.13 = (bf16[512,512]{1,0:T(8,128)(2,1)S(1)}, bf16[512,512]{1,0:T(8,128)(2,1)S(1)}, u32[]{:S(2)}, u32[]{:S(2)}) collective-permute-start(bf16[512,512]{1,0:T(8,128)(2,1)S(1)} %collective-permute-done.12), channel_id=1, source_target_pairs={{0,4},{2,6},{4,0},{6,2},{8,12},{10,14},{12,8},{14,10},{16,20},{18,... | collective-permute-start | bytes 1572872 | tf_op jit(solution)/shard_map/ppermute | solution.py:26
  100.0 36.8 %collective-permute-start.8 = (bf16[512,512]{1,0:T(8,128)(2,1)S(1)}, bf16[512,512]{1,0:T(8,128)(2,1)S(1)}, u32[]{:S(2)}, u32[]{:S(2)}) collective-permute-start(bf16[512,512]{1,0:T(8,128)(2,1)S(1)} %collective-permute-done.6), channel_id=1, source_target_pairs={{0,8},{2,10},{4,12},{6,14},{8,16},{10,18},{12,20},{14,22},{16,24},... | collective-permute-start | bytes 1572872 | tf_op jit(solution)/shard_map/ppermute | solution.py:31
  100.6 28.5 %collective-permute-start.7 = (bf16[512,512]{1,0:T(8,128)(2,1)S(1)}, bf16[512,512]{1,0:T(8,128)(2,1)S(1)}, u32[]{:S(2)}, u32[]{:S(2)}) collective-permute-start(bf16[512,512]{1,0:T(8,128)(2,1)S(1)} %collective-permute-done.6), channel_id=1, source_target_pairs={{0,4},{2,6},{4,0},{6,2},{8,12},{10,14},{12,8},{14,10},{16,20},{18,... | collective-permute-start | bytes 1572872 | tf_op jit(solution)/shard_map/ppermute | solution.py:26
  111.2 25.1 %collective-permute-start.16 = (bf16[512,512]{1,0:T(8,128)(2,1)S(1)}, bf16[512,512]{1,0:T(8,128)(2,1)S(1)}, u32[]{:S(2)}, u32[]{:S(2)}) collective-permute-start(bf16[512,512]{1,0:T(8,128)(2,1)S(1)} %collective-permute-done.14), channel_id=1, source_target_pairs={{0,8},{2,10},{4,12},{6,14},{8,16},{10,18},{12,20},{14,22},{16,24},... | collective-permute-start | bytes 1572872 | tf_op jit(solution)/shard_map/ppermute | solution.py:31
  113.7 35.5 %collective-permute-start.15 = (bf16[512,512]{1,0:T(8,128)(2,1)S(1)}, bf16[512,512]{1,0:T(8,128)(2,1)S(1)}, u32[]{:S(2)}, u32[]{:S(2)}) collective-permute-start(bf16[512,512]{1,0:T(8,128)(2,1)S(1)} %collective-permute-done.14), channel_id=1, source_target_pairs={{0,4},{2,6},{4,0},{6,2},{8,12},{10,14},{12,8},{14,10},{16,20},{18,... | collective-permute-start | bytes 1572872 | tf_op jit(solution)/shard_map/ppermute | solution.py:26
  129.1 19.6 %collective-permute-start.9 = (bf16[512,512]{1,0:T(8,128)(2,1)S(1)}, bf16[512,512]{1,0:T(8,128)(2,1)S(1)}, u32[]{:S(2)}, u32[]{:S(2)}) collective-permute-start(bf16[512,512]{1,0:T(8,128)(2,1)S(1)} %collective-permute-done.7), channel_id=1, source_target_pairs={{0,8},{2,10},{4,12},{6,14},{8,16},{10,18},{12,20},{14,22},{16,24},... | collective-permute-start | bytes 1572872 | tf_op jit(solution)/shard_map/ppermute | solution.py:31
  136.3 15.3 %collective-permute-start.17 = (bf16[512,512]{1,0:T(8,128)(2,1)S(1)}, bf16[512,512]{1,0:T(8,128)(2,1)S(1)}, u32[]{:S(2)}, u32[]{:S(2)}) collective-permute-start(bf16[512,512]{1,0:T(8,128)(2,1)S(1)} %collective-permute-done.16), channel_id=1, source_target_pairs={{0,4},{2,6},{4,0},{6,2},{8,12},{10,14},{12,8},{14,10},{16,20},{18,... | collective-permute-start | bytes 1572872 | tf_op jit(solution)/shard_map/ppermute | solution.py:26
  149.6 7.0 %copy-start.14 = (bf16[896,2048]{1,0:T(8,128)(2,1)S(1)}, bf16[896,2048]{1,0:T(8,128)(2,1)}, u32[]{:S(2)}) copy-start(bf16[896,2048]{1,0:T(8,128)(2,1)} %param.15) | copy-start | bytes 11010052
  152.1 11.7 %collective-permute-start.18 = (bf16[256,1024]{1,0:T(8,128)(2,1)S(1)}, bf16[256,1024]{1,0:T(8,128)(2,1)S(1)}, u32[]{:S(2)}, u32[]{:S(2)}) collective-permute-start(bf16[256,1024]{1,0:T(8,128)(2,1)S(1)} %pad_maximum_fusion.6), channel_id=1, source_target_pairs={{0,2},{2,0},{4,6},{6,4},{8,10},{10,8},{12,14},{14,12},{16,18},{18,... | collective-permute-start | bytes 1572872 | tf_op jit(solution)/shard_map/ppermute | solution.py:26
  192.7 1.2 copy-start.5
  193.1 32.2 %copy-start.4 = (bf16[256,2048]{1,0:T(8,128)(2,1)}, bf16[256,2048]{1,0:T(8,128)(2,1)S(1)}, u32[]{:S(2)}) copy-start(bf16[256,2048]{1,0:T(8,128)(2,1)S(1)} %slice_select_fusion) | copy-start | bytes 3145732
  193.1 32.2 %collective-permute-start.22 = (bf16[256,2048]{1,0:T(8,128)(2,1)S(1)}, bf16[256,2048]{1,0:T(8,128)(2,1)S(1)}, u32[]{:S(2)}, u32[]{:S(2)}) collective-permute-start(bf16[256,2048]{1,0:T(8,128)(2,1)S(1)} %slice_select_fusion), channel_id=1, source_target_pairs={{0,2},{2,0},{4,6},{6,4},{8,10},{10,8},{12,14},{14,12},{16,18},{18,... | collective-permute-start | bytes 3145736 | tf_op jit(solution)/shard_map/ppermute | solution.py:26
  195.0 18.0 %collective-permute-start.28 = (bf16[1024,256]{1,0:T(8,128)(2,1)}, bf16[1024,256]{1,0:T(8,128)(2,1)}, u32[]{:S(2)}, u32[]{:S(2)}) collective-permute-start(bf16[1024,256]{1,0:T(8,128)(2,1)} %get-tuple-element.26), channel_id=1, source_target_pairs={{0,8},{2,10},{4,12},{6,14},{8,16},{10,18},{12,20},{14,22},{16,24},... | collective-permute-start | bytes 1572872 | tf_op jit(solution)/shard_map/ppermute | solution.py:31
  198.0 26.3 %collective-permute-start.26 = (bf16[1024,256]{1,0:T(8,128)(2,1)}, bf16[1024,256]{1,0:T(8,128)(2,1)}, u32[]{:S(2)}, u32[]{:S(2)}) collective-permute-start(bf16[1024,256]{1,0:T(8,128)(2,1)} %get-tuple-element.25), channel_id=1, source_target_pairs={{0,8},{2,10},{4,12},{6,14},{8,16},{10,18},{12,20},{14,22},{16,24},... | collective-permute-start | bytes 1572872 | tf_op jit(solution)/shard_map/ppermute | solution.py:31
  199.5 47.8 %collective-permute-start.24 = (bf16[1024,256]{1,0:T(8,128)(2,1)}, bf16[1024,256]{1,0:T(8,128)(2,1)}, u32[]{:S(2)}, u32[]{:S(2)}) collective-permute-start(bf16[1024,256]{1,0:T(8,128)(2,1)} %get-tuple-element.26), channel_id=1, source_target_pairs={{0,4},{2,6},{4,0},{6,2},{8,12},{10,14},{12,8},{14,10},{16,20},{18,... | collective-permute-start | bytes 1572872 | tf_op jit(solution)/shard_map/ppermute | solution.py:26
  200.4 71.7 %collective-permute-start.23 = (bf16[1024,256]{1,0:T(8,128)(2,1)}, bf16[1024,256]{1,0:T(8,128)(2,1)}, u32[]{:S(2)}, u32[]{:S(2)}) collective-permute-start(bf16[1024,256]{1,0:T(8,128)(2,1)} %get-tuple-element.25), channel_id=1, source_target_pairs={{0,4},{2,6},{4,0},{6,2},{8,12},{10,14},{12,8},{14,10},{16,20},{18,... | collective-permute-start | bytes 1572872 | tf_op jit(solution)/shard_map/ppermute | solution.py:26
  201.6 26.5 %copy-start.6 = (bf16[2048,256]{1,0:T(8,128)(2,1)S(1)}, bf16[2048,256]{1,0:T(8,128)(2,1)}, u32[]{:S(2)}) copy-start(bf16[2048,256]{1,0:T(8,128)(2,1)} %param.19) | copy-start | bytes 3145732
  213.1 22.4 %collective-permute-start.29 = (bf16[1024,256]{1,0:T(8,128)(2,1)}, bf16[1024,256]{1,0:T(8,128)(2,1)S(1)}, u32[]{:S(2)}, u32[]{:S(2)}) collective-permute-start(bf16[1024,256]{1,0:T(8,128)(2,1)} %collective-permute-done.28), channel_id=1, source_target_pairs={{0,8},{2,10},{4,12},{6,14},{8,16},{10,18},{12,20},{14,22},{16,24},... | collective-permute-start | bytes 1572872 | tf_op jit(solution)/shard_map/ppermute | solution.py:31
  224.3 54.1 %collective-permute-start.35 = (bf16[1024,256]{1,0:T(8,128)(2,1)}, bf16[1024,256]{1,0:T(8,128)(2,1)S(1)}, u32[]{:S(2)}, u32[]{:S(2)}) collective-permute-start(bf16[1024,256]{1,0:T(8,128)(2,1)} %collective-permute-done.28), channel_id=1, source_target_pairs={{0,4},{2,6},{4,0},{6,2},{8,12},{10,14},{12,8},{14,10},{16,20},{18,... | collective-permute-start | bytes 1572872 | tf_op jit(solution)/shard_map/ppermute | solution.py:26
  225.3 1.0 copy-start.8
  226.4 20.0 %collective-permute-start.27 = (bf16[1024,256]{1,0:T(8,128)(2,1)}, bf16[1024,256]{1,0:T(8,128)(2,1)S(1)}, u32[]{:S(2)}, u32[]{:S(2)}) collective-permute-start(bf16[1024,256]{1,0:T(8,128)(2,1)} %collective-permute-done.26), channel_id=1, source_target_pairs={{0,8},{2,10},{4,12},{6,14},{8,16},{10,18},{12,20},{14,22},{16,24},... | collective-permute-start | bytes 1572872 | tf_op jit(solution)/shard_map/ppermute | solution.py:31
  235.4 45.1 %collective-permute-start.34 = (bf16[1024,256]{1,0:T(8,128)(2,1)}, bf16[1024,256]{1,0:T(8,128)(2,1)S(1)}, u32[]{:S(2)}, u32[]{:S(2)}) collective-permute-start(bf16[1024,256]{1,0:T(8,128)(2,1)} %collective-permute-done.26), channel_id=1, source_target_pairs={{0,4},{2,6},{4,0},{6,2},{8,12},{10,14},{12,8},{14,10},{16,20},{18,... | collective-permute-start | bytes 1572872 | tf_op jit(solution)/shard_map/ppermute | solution.py:26
  246.4 14.8 %collective-permute-start.31 = (bf16[1024,256]{1,0:T(8,128)(2,1)S(1)}, bf16[1024,256]{1,0:T(8,128)(2,1)S(1)}, u32[]{:S(2)}, u32[]{:S(2)}) collective-permute-start(bf16[1024,256]{1,0:T(8,128)(2,1)S(1)} %collective-permute-done.29), channel_id=1, source_target_pairs={{0,4},{2,6},{4,0},{6,2},{8,12},{10,14},{12,8},{14,10},{16,20},{18,... | collective-permute-start | bytes 1572872 | tf_op jit(solution)/shard_map/ppermute | solution.py:26
  247.4 24.2 %collective-permute-start.30 = (bf16[1024,256]{1,0:T(8,128)(2,1)S(1)}, bf16[1024,256]{1,0:T(8,128)(2,1)S(1)}, u32[]{:S(2)}, u32[]{:S(2)}) collective-permute-start(bf16[1024,256]{1,0:T(8,128)(2,1)S(1)} %collective-permute-done.27), channel_id=1, source_target_pairs={{0,4},{2,6},{4,0},{6,2},{8,12},{10,14},{12,8},{14,10},{16,20},{18,... | collective-permute-start | bytes 1572872 | tf_op jit(solution)/shard_map/ppermute | solution.py:26
  261.2 14.0 %collective-permute-start.38 = (bf16[1024,256]{1,0:T(8,128)(2,1)S(1)}, bf16[1024,256]{1,0:T(8,128)(2,1)S(1)}, u32[]{:S(2)}, u32[]{:S(2)}) collective-permute-start(bf16[1024,256]{1,0:T(8,128)(2,1)S(1)} %collective-permute-done.29), channel_id=1, source_target_pairs={{0,8},{2,10},{4,12},{6,14},{8,16},{10,18},{12,20},{14,22},{16,24},... | collective-permute-start | bytes 1572872 | tf_op jit(solution)/shard_map/ppermute | solution.py:31
  271.5 16.7 %collective-permute-start.37 = (bf16[1024,256]{1,0:T(8,128)(2,1)S(1)}, bf16[1024,256]{1,0:T(8,128)(2,1)S(1)}, u32[]{:S(2)}, u32[]{:S(2)}) collective-permute-start(bf16[1024,256]{1,0:T(8,128)(2,1)S(1)} %collective-permute-done.27), channel_id=1, source_target_pairs={{0,8},{2,10},{4,12},{6,14},{8,16},{10,18},{12,20},{14,22},{16,24},... | collective-permute-start | bytes 1572872 | tf_op jit(solution)/shard_map/ppermute | solution.py:31
  272.0 25.6 %collective-permute-start.39 = (bf16[1024,256]{1,0:T(8,128)(2,1)S(1)}, bf16[1024,256]{1,0:T(8,128)(2,1)S(1)}, u32[]{:S(2)}, u32[]{:S(2)}) collective-permute-start(bf16[1024,256]{1,0:T(8,128)(2,1)S(1)} %collective-permute-done.30), channel_id=1, source_target_pairs={{0,8},{2,10},{4,12},{6,14},{8,16},{10,18},{12,20},{14,22},{16,24},... | collective-permute-start | bytes 1572872 | tf_op jit(solution)/shard_map/ppermute | solution.py:31
  275.2 13.6 %collective-permute-start.40 = (bf16[1024,256]{1,0:T(8,128)(2,1)S(1)}, bf16[1024,256]{1,0:T(8,128)(2,1)S(1)}, u32[]{:S(2)}, u32[]{:S(2)}) collective-permute-start(bf16[1024,256]{1,0:T(8,128)(2,1)S(1)} %collective-permute-done.38), channel_id=1, source_target_pairs={{0,4},{2,6},{4,0},{6,2},{8,12},{10,14},{12,8},{14,10},{16,20},{18,... | collective-permute-start | bytes 1572872 | tf_op jit(solution)/shard_map/ppermute | solution.py:26
  278.4 19.8 %collective-permute-start.25 = (bf16[256,512]{0,1:T(8,128)(2,1)S(1)}, bf16[256,512]{0,1:T(8,128)(2,1)S(1)}, u32[]{:S(2)}, u32[]{:S(2)}) collective-permute-start(bf16[256,512]{0,1:T(8,128)(2,1)S(1)} %pad_maximum_fusion.13), channel_id=1, source_target_pairs={{0,2},{2,0},{4,6},{6,4},{8,10},{10,8},{12,14},{14,12},{16,18},{18,... | collective-permute-start | bytes 786440 | tf_op jit(solution)/shard_map/ppermute | solution.py:26
  280.5 17.8 %collective-permute-start.32 = (bf16[256,512]{0,1:T(8,128)(2,1)S(1)}, bf16[256,512]{0,1:T(8,128)(2,1)S(1)}, u32[]{:S(2)}, u32[]{:S(2)}) collective-permute-start(bf16[256,512]{0,1:T(8,128)(2,1)S(1)} %pad_maximum_fusion.16), channel_id=1, source_target_pairs={{0,2},{2,0},{4,6},{6,4},{8,10},{10,8},{12,14},{14,12},{16,18},{18,... | collective-permute-start | bytes 786440 | tf_op jit(solution)/shard_map/ppermute | solution.py:26
  288.2 12.1 %collective-permute-start.36 = (bf16[256,512]{0,1:T(8,128)(2,1)S(1)}, bf16[256,512]{0,1:T(8,128)(2,1)S(1)}, u32[]{:S(2)}, u32[]{:S(2)}) collective-permute-start(bf16[256,512]{0,1:T(8,128)(2,1)S(1)} %pad_maximum_fusion.19), channel_id=1, source_target_pairs={{0,2},{2,0},{4,6},{6,4},{8,10},{10,8},{12,14},{14,12},{16,18},{18,... | collective-permute-start | bytes 786440 | tf_op jit(solution)/shard_map/ppermute | solution.py:26
  298.1 2.1 collective-permute-start.41
  298.7 14.8 %collective-permute-start.33 = (bf16[256,1024]{0,1:T(8,128)(2,1)S(1)}, bf16[256,1024]{0,1:T(8,128)(2,1)S(1)}, u32[]{:S(2)}, u32[]{:S(2)}) collective-permute-start(bf16[256,1024]{0,1:T(8,128)(2,1)S(1)} %broadcast_select_fusion.6), channel_id=1, source_target_pairs={{0,1},{1,0},{2,3},{3,2},{4,5},{5,4},{6,7},{7,6},{8,9},{9,8},{10,11... | collective-permute-start | bytes 1572872 | tf_op jit(solution)/shard_map/ppermute | solution.py:26
  300.7 23.6 %collective-permute-start.42 = (bf16[256,1024]{0,1:T(8,128)(2,1)S(1)}, bf16[256,1024]{0,1:T(8,128)(2,1)S(1)}, u32[]{:S(2)}, u32[]{:S(2)}) collective-permute-start(bf16[256,1024]{0,1:T(8,128)(2,1)S(1)} %broadcast_select_fusion.3), channel_id=1, source_target_pairs={{0,1},{1,0},{2,3},{3,2},{4,5},{5,4},{6,7},{7,6},{8,9},{9,8},{10,11... | collective-permute-start | bytes 1572872 | tf_op jit(solution)/shard_map/ppermute | solution.py:26
  329.8 6.2 %copy-start.1 = (bf16[1792,896]{1,0:T(8,128)(2,1)S(1)}, bf16[1792,896]{1,0:T(8,128)(2,1)}, u32[]{:S(2)}) copy-start(bf16[1792,896]{1,0:T(8,128)(2,1)} %param.14) | copy-start | bytes 9633796

commit v2 on v0

v2 whole, which is shorter than its diff:
```python
import functools

import jax
import jax.numpy as jnp
from jax import lax
from jax.experimental import pallas as pl
from jax.experimental.pallas import tpu as pltpu
from jax.sharding import PartitionSpec as P

HD = 128
M = 64
KEYS = 256


def factors(count):
    core = 2 if count % 2 == 0 else 1
    y = 2 if (count // core) % 2 == 0 else 1
    return count // (core * y), y, core


def swap(value, axis, stride):
    count = lax.axis_size(axis)
    pairs = [(i, i + stride if (i // stride) % 2 == 0 else i - stride) for i in range(count)]
    return lax.ppermute(value, axis, pairs)


def ring(value, axis, stride):
    count = lax.axis_size(axis)
    return lax.ppermute(value, axis, [(i, (i + stride) % count) for i in range(count)])


def named(name):
    def wrap(function):
        def inner(*args):
            with jax.named_scope(name):
                return function(*args)

        return inner

    return wrap


def after(value, *done):
    return lax.optimization_barrier((value,) + done)[0]


class Stream:
    def __init__(self, name, block):
        self.depth, self.n_y, self.n_core = factors(lax.axis_size("seq"))
        self.name, self.blocks = name, {(0, 0): block}

    def fetch(self, k, j, way, mark):
        step = self.n_core * self.n_y
        with jax.named_scope(f"{self.name}_{k}_{j}"):
            if way == "y":
                made = swap(after(self.blocks[k, 0], *mark), "seq", self.n_core)
            elif way == "on":
                made = ring(after(self.blocks[k - 1, j], *mark), "seq", step)
            else:
                made = ring(after(self.blocks[(k + 1) % self.depth, j], *mark), "seq", -step)
        self.blocks[k, j] = made


def ordered(flag, first, second, axis):
    return jnp.concatenate(
        [jnp.where(flag, first, second), jnp.where(flag, second, first)], axis=axis
    )


WHOLE = pl.BlockSpec(memory_space=pltpu.VMEM)
SCALARS = pl.BlockSpec(memory_space=pltpu.SMEM)


def cost(flops, moved):
    return pl.CostEstimate(flops=int(flops), bytes_accessed=int(moved), transcendentals=0)


def params(mib):
    return pltpu.CompilerParams(vmem_limit_bytes=mib * 1024 * 1024)


def tiles(size, tile=256):
    return tile if size % tile == 0 else size


def encode_kernel(x_ref, gain_ref, first_ref, second_ref, out_ref, norm_ref, inner_ref):
    x = x_ref[...].astype(jnp.float32)
    scale = lax.rsqrt(jnp.mean(x * x, axis=-1, keepdims=True) + 1e-06)
    norm_ref[...] = (x * scale * gain_ref[...]).astype(jnp.bfloat16)
    units = first_ref.shape[1]
    tile = tiles(units)
    for n in range(0, units, tile):
        made = jnp.dot(norm_ref[...], first_ref[:, n : n + tile], preferred_element_type=jnp.float32)
        inner_ref[:, n : n + tile] = jnp.maximum(made, 0.0).astype(jnp.bfloat16)
    rows = tiles(x_ref.shape[0])
    for m in range(0, x_ref.shape[0], rows):
        out_ref[m : m + rows, :] = jnp.dot(
            inner_ref[m : m + rows, :], second_ref[...], preferred_element_type=jnp.float32
        ).astype(jnp.bfloat16)


def encode_partial(tokens, gain, first_weight, second_weight):
    rows = tokens.shape[0]
    return pl.pallas_call(
        encode_kernel,
        in_specs=[WHOLE] * 4,
        out_specs=WHOLE,
        out_shape=jax.ShapeDtypeStruct((rows, second_weight.shape[1]), jnp.bfloat16),
        scratch_shapes=[
            pltpu.VMEM(tokens.shape, jnp.bfloat16),
            pltpu.VMEM((rows, first_weight.shape[1]), jnp.bfloat16),
        ],
        compiler_params=params(14),
        cost_estimate=cost(4 * rows * tokens.shape[1] * first_weight.shape[1], 4 * first_weight.size),
        name="encode",
    )(tokens, gain, first_weight, second_weight)


def project_kernel(terms, *refs):
    part_refs, (k_in, v_in, enc_ref, k_ref, v_ref) = refs[:terms], refs[terms:]
    total = part_refs[0][...].astype(jnp.float32)
    if terms > 1:
        summed = part_refs[1][...].astype(jnp.float32)
        for ref in part_refs[2:]:
            summed = summed + ref[...].astype(jnp.float32)
        total = total + summed
    enc_ref[...] = total.astype(jnp.bfloat16)
    cols = k_in.shape[1]
    tile = tiles(cols)
    for w_ref, o_ref in ((k_in, k_ref), (v_in, v_ref)):
        for n in range(0, cols, tile):
            o_ref[:, n : n + tile] = jnp.dot(
                enc_ref[...], w_ref[:, n : n + tile], preferred_element_type=jnp.float32
            ).astype(jnp.bfloat16)


def project(parts, key_weight, value_weight):
    rows, width = parts[0].shape
    cols = key_weight.shape[1]
    return pl.pallas_call(
        functools.partial(project_kernel, len(parts)),
        in_specs=[WHOLE] * (len(parts) + 2),
        out_specs=[WHOLE] * 3,
        out_shape=[
            jax.ShapeDtypeStruct((rows, width), jnp.bfloat16),
            jax.ShapeDtypeStruct((rows, cols), jnp.bfloat16),
            jax.ShapeDtypeStruct((rows, cols), jnp.bfloat16),
        ],
        compiler_params=params(18),
        cost_estimate=cost(4 * rows * width * cols, 4 * key_weight.size),
        name="project",
    )(*parts, key_weight, value_weight)


def decode_kernel(at_ref, own_ref, came_ref, gain_ref, out_ref):
    own, came = own_ref[...].astype(jnp.float32), came_ref[...].astype(jnp.float32)
    shards, _, width = out_ref.shape
    half = shards // 2
    total = jnp.sum(own * own, axis=-1, keepdims=True) + jnp.sum(came * came, axis=-1, keepdims=True)
    scale = lax.rsqrt(total / (shards * width) + 1e-06)
    for i, ref in enumerate((own_ref, came_ref)):
        for g in range(half):
            to = at_ref[i] + g
            value = ref[:, g * width : (g + 1) * width].astype(jnp.float32)
            out_ref[to] = (value * scale * gain_ref[to]).astype(jnp.bfloat16)


def decode_norm(own_first, own, came, gain, shards):
    rows, half = own.shape
    width = 2 * half // shards
    at = jnp.where(own_first, jnp.array([0, shards // 2]), jnp.array([shards // 2, 0]))
    return pl.pallas_call(
        decode_kernel,
        in_specs=[SCALARS] + [WHOLE] * 3,
        out_specs=WHOLE,
        out_shape=jax.ShapeDtypeStruct((shards, rows, width), jnp.bfloat16),
        compiler_params=params(8),
        cost_estimate=cost(0, 10 * own.size),
        name="decode",
    )(at.astype(jnp.int32), own, came, gain.reshape(shards, 1, width))


def query_kernel(norms, blocks, more, at_ref, *refs):
    norm_refs, block_refs = refs[:norms], refs[norms : norms + blocks]
    out_ref = refs[-1]
    rows, depth = norm_refs[0].shape[1:]
    tile = tiles(out_ref.shape[1])
    for i, norm_ref in enumerate(norm_refs):
        own = slice(i * rows, (i + 1) * rows)
        for n in range(0, out_ref.shape[1], tile):
            cols = slice(n, n + tile)
            total, at = None, 0
            for block_ref in block_refs:
                for first in range(0, block_ref.shape[0], depth):
                    term = jnp.dot(
                        norm_ref[at_ref[at]],
                        block_ref[first : first + depth, cols],
                        preferred_element_type=jnp.float32,
                    )
                    total, at = term if total is None else total + term, at + 1
            if more:
                total = total + refs[-2][own, cols]
            out_ref[own, cols] = total.astype(out_ref.dtype)


def add_query(at, norms, blocks, total, dtype):
    more = () if total is None else (total,)
    shape = (len(norms) * norms[0].shape[1], blocks[0].shape[1])
    moved = sum(b.size for b in blocks)
    return pl.pallas_call(
        functools.partial(query_kernel, len(norms), len(blocks), len(more)),
        in_specs=[SCALARS] + [WHOLE] * (len(norms) + len(blocks) + len(more)),
        out_specs=WHOLE,
        out_shape=jax.ShapeDtypeStruct(shape, dtype),
        compiler_params=params(18),
        cost_estimate=cost(2 * shape[0] * moved, 2 * moved),
        name="query",
    )(at, *norms, *blocks, *more)


def out_kernel(attns, sizes, near_ref, *refs):
    attn_refs, block_refs, out_refs = refs[:attns], refs[attns:-attns], refs[-attns:]
    first = 0
    for i, counts in enumerate(sizes):
        for branch, count in enumerate(counts):
            parts = block_refs[first : first + count]
            first += count

            @pl.when(near_ref[i] == 1 - branch)
            def _(i=i, parts=parts):
                for attn_ref, out_ref in zip(attn_refs, out_refs):
                    total, row = None, 0
                    for ref in parts:
                        size = ref.shape[0]
                        term = jnp.dot(
                            attn_ref[:, row : row + size],
                            ref[...],
                            preferred_element_type=jnp.float32,
                        )
                        total, row = term if total is None else total + term, row + size
                    out_ref[i] = total.astype(jnp.bfloat16)


def out_products(near, attns, pairs):
    shape = jax.ShapeDtypeStruct(
        (len(pairs), attns[0].shape[0], pairs[0][0][0].shape[1]), jnp.bfloat16
    )
    flat = [part for pair in pairs for block in pair for part in block]
    return pl.pallas_call(
        functools.partial(out_kernel, len(attns), [[len(b) for b in pair] for pair in pairs]),
        in_specs=[SCALARS] + [WHOLE] * (len(attns) + len(flat)),
        out_specs=[WHOLE] * len(attns),
        out_shape=[shape] * len(attns),
        compiler_params=params(14),
        cost_estimate=cost(0, 1024),
        name="out",
    )(near, *attns, *flat)


def attend_kernel(heads, pieces, q_ref, *refs):
    k_refs, v_refs, o_ref = refs[: len(pieces)], refs[len(pieces) : -1], refs[-1]
    scale = HD ** (-0.5)
    units = [(p, s) for p, count in enumerate(pieces) for s in range(count)]
    for h in range(heads):
        cols = slice(h * HD, (h + 1) * HD)
        scores = []
        for u, (p, s) in enumerate(units):
            scores.append(
                lax.dot_general(
                    q_ref[u * M : (u + 1) * M, cols],
                    k_refs[p][s * KEYS : (s + 1) * KEYS, cols],
                    (((1,), (1,)), ((), ())),
                    preferred_element_type=jnp.float32,
                )
            )
        tops = [jnp.max(s, axis=-1, keepdims=True) for s in scores]
        exps = [jnp.exp((s - t) * scale) for s, t in zip(scores, tops)]
        scales = [1.0 / jnp.sum(e, axis=-1, keepdims=True) for e in exps]
        probs = [(e * r).astype(jnp.bfloat16) for e, r in zip(exps, scales)]
        for u, (p, s) in enumerate(units):
            o_ref[u * M : (u + 1) * M, cols] = jnp.dot(
                probs[u],
                v_refs[p][s * KEYS : (s + 1) * KEYS, cols],
                preferred_element_type=jnp.float32,
            ).astype(jnp.bfloat16)


def attend(query, keys, values):
    rows, width = query.shape
    heads = 2 if (width // HD) % 2 == 0 else 1
    block = heads * HD
    pieces = tuple(k.shape[0] // KEYS for k in keys)
    held = [pl.BlockSpec((k.shape[0], block), lambda i: (0, i)) for k in keys]
    return pl.pallas_call(
        functools.partial(attend_kernel, heads, pieces),
        grid=(width // block,),
        in_specs=[pl.BlockSpec((rows, block), lambda i: (0, i))] + held + held,
        out_specs=pl.BlockSpec((rows, block), lambda i: (0, i)),
        out_shape=jax.ShapeDtypeStruct((rows, width), jnp.bfloat16),
        compiler_params=params(10),
        cost_estimate=cost(0, 1024),
        name="attend",
    )(query, *keys, *values)


def per_device(
    hidden,
    neighbours,
    enc_gain,
    enc_w1,
    enc_w2,
    key_weight,
    value_weight,
    dec_gain,
    query_weight,
    out_weight,
):
    tok_rows, feat = hidden.shape
    span_count, key_rows, width = neighbours.shape
    n_seq, n_tp = lax.axis_size("seq"), lax.axis_size("tp")
    depth, n_y, n_core = factors(n_seq)
    me = lax.axis_index("seq")
    tp_at = lax.axis_index("tp")
    core_at, y_at, z_at = me % n_core, (me // n_core) % n_y, me // (n_core * n_y)
    core_first = core_at == 0

    q_rows, q_cols = query_weight.shape
    per_core = q_cols // n_core
    block = lax.dynamic_slice(query_weight, (0, core_at * per_core), (q_rows, per_core))
    if n_core == 2:
        theirs = lax.dynamic_slice(query_weight, (0, (1 - core_at) * per_core), (q_rows, per_core))
        block = jnp.concatenate([block, swap(theirs, "seq", 1)], axis=0)
    q_stream = Stream("query", block)

    o_rows, o_cols = out_weight.shape
    o_stream = Stream("out", out_weight)

    if n_tp == 2:
        hidden_came = swap(hidden, "tp", 1)
    else:
        hidden_came = lax.all_gather(hidden, "tp", axis=1, tiled=True)

    flat = neighbours.reshape(span_count * key_rows, width)
    piece_rows = flat.shape[0] // 2
    parts = [flat[i * piece_rows : (i + 1) * piece_rows] for i in range(2)]
    gain = enc_gain.reshape(1, width)
    v = {}

    @named("encode")
    def encode(i, mark):
        v["part", i] = encode_partial(after(parts[i], *mark), gain, enc_w1, enc_w2)
        return (v["part", i],)

    @named("encode_sum")
    def encode_sum(i, mark):
        own = after(v["part", i], *mark)
        if n_tp == 2:
            v["sum", i] = (own, swap(own, "tp", 1))
        else:
            v["sum", i] = (lax.psum(own, "tp"),)
        return v["sum", i]

    @named("decode")
    def decode(mark):
        came = after(hidden_came, *mark)
        if n_tp == 2:
            norm = decode_norm(tp_at == 0, hidden, came, dec_gain, n_seq)
        else:
            wide = came.astype(jnp.float32)
            norm = wide * lax.rsqrt(jnp.mean(wide * wide, axis=-1, keepdims=True) + 1e-06) * dec_gain
            norm = norm.astype(jnp.bfloat16).reshape(tok_rows, n_seq, q_rows)
            norm = jnp.moveaxis(norm, 1, 0)
        v["norm"] = (norm, swap(norm, "seq", 1)) if n_core == 2 else (norm,)
        return (norm,)

    @named("keys_values")
    def keys_values(i, mark):
        terms = tuple(after(t, *mark) for t in v["sum", i])
        encoded, *v["kv", i] = project((parts[i],) + terms, key_weight, value_weight)
        if i == 1:
            v["earlier"] = lax.ppermute(
                encoded[piece_rows - key_rows :], "seq", [(i, i + 1) for i in range(n_seq - 1)]
            )
        return tuple(v["kv", i])

    @named("keys_values_earlier")
    def keys_values_earlier(mark):
        v["kv", 2] = project((after(v["earlier"], *mark),), key_weight, value_weight)[1:]
        return tuple(v["kv", 2])

    @named("query_part")
    def query_part(keys, last, mark):
        at = [
            (((z_at - k) % depth) * n_y + (y_at + j) % n_y) * n_core + (core_at + c) % n_core
            for k, j in keys
            for c in range(n_core)
        ]
        norms = tuple(after(n, *mark) for n in v["norm"])
        v["q"] = add_query(
            jnp.stack(at).astype(jnp.int32),
            norms,
            [q_stream.blocks[key] for key in keys],
            v.get("q"),
            jnp.bfloat16 if last else jnp.float32,
        )
        return (v["q"],)

    @named("attention")
    def attention(mark):
        query = v["q"]
        if n_core == 2:
            query = ordered(core_first, query[:tok_rows], swap(query[tok_rows:], "seq", 1), 1)
        grouped = jnp.pad(query, ((1, M - 1), (0, 0)))
        keys, values = zip(v["kv", 2], v["kv", 0], v["kv", 1])
        attn = attend(grouped, keys, values)[1 : tok_rows + 1]
        position = me * tok_rows + jnp.arange(tok_rows, dtype=jnp.int32)[:, None]
        attn = jnp.where(position >= M - 1, attn, jnp.zeros_like(attn))
        v["attn"] = (attn, swap(attn, "seq", 1)) if n_core == 2 else (attn,)
        return (attn,)

    pairs = depth // 2

    @named("scatter")
    def scatter(keys, mark):
        stay = jnp.stack(
            [(((z_at - p) % depth) // pairs == tp_at).astype(jnp.int32) for p, j in keys]
        )
        attns = tuple(after(a, *mark) for a in v["attn"])
        blocks = [((o_stream.blocks[p, j],), (o_stream.blocks[p + pairs, j],)) for p, j in keys]
        sent = out_products(1 - stay, attns, blocks)
        if n_core == 2:
            sent = (sent[0], swap(sent[1], "seq", 1))
        kept = out_products(stay, tuple(after(a, *sent) for a in attns), blocks)
        if n_core == 2:
            kept = (kept[0], swap(kept[1], "seq", 1))
        came = swap(jnp.concatenate(sent, axis=0), "tp", 1)
        for i, key in enumerate(keys):
            v[("piece",) + key] = [
                (kept[c][i], came[c * len(keys) + i]) for c in range(n_core)
            ]
        return (came,) + tuple(kept)

    scatters = n_tp == 2 and depth % 4 == 0
    q, o = q_stream, o_stream
    if depth == 4 and n_y == 2:
        plan = [
            [(q, 1, 0, "on"), (q, 0, 1, "y"), (q, 3, 0, "back"), (o, 0, 1, "y")],
            [(q, 2, 0, "on"), (q, 1, 1, "y"), (o, 1, 0, "on"), (q, 3, 1, "y")],
            [(o, 2, 0, "on"), (q, 2, 1, "y")],
            [(o, 3, 0, "back"), (o, 1, 1, "y")],
            [(o, 3, 1, "back"), (o, 2, 1, "y")],
        ]
    else:
        plan = []
        for k in range(1, depth + 1):
            plan.append([(s, k, 0, "on") for s in (q, o) if k < depth])
            plan[-1] += [(s, k - 1, 1, "y") for s in (q, o) if n_y == 2]
        plan.append([])
    last_query = 1 + max(i for i, moves in enumerate(plan) if any(m[0] is q for m in moves))
    arrived = [(q, 0, 0), (o, 0, 0)]
    asked, made = set(), set()
    token = after(jnp.float32(0), q.blocks[0, 0])
    for phase, moves in enumerate(plan):
        mark = (token,) if phase else ()
        for s, k, j, way in moves:
            s.fetch(k, j, way, mark)
        mark = (token,)
        values = ()
        if phase == 0:
            values += encode(0, mark) + encode_sum(0, mark) + encode(1, mark) + (hidden_came,)
        elif phase == 1:
            values += decode(mark) + keys_values(0, mark) + encode_sum(1, v["norm"])
        elif phase == 2:
            values += keys_values(1, mark)
        elif phase == 3:
            values += keys_values_earlier(mark)
        if 1 <= phase <= last_query:
            keys = [(k, j) for s, k, j in arrived if s is q and (k, j) not in asked]
            asked.update(keys)
            values += query_part(keys, phase == last_query, mark)
        if phase == last_query:
            values += attention(mark)
        if phase > last_query and scatters:
            keys = [(p, j) for p in range(pairs) for j in range(n_y)]
            keys = [
                key
                for key in keys
                if key not in made and {(o,) + key, (o, key[0] + pairs, key[1])} <= set(arrived)
            ]
            if keys:
                made.update(keys)
                values += scatter(keys, mark)
        arrived += [m[:3] for m in moves]
        token = after(token, *(s.blocks[k, j] for s, k, j, _ in moves), *values)

    if scatters:
        order = [(p, j) for p in range(pairs) for j in range(n_y)]
        rest = [key for key in order if key not in made]
        if rest:
            scatter(rest, (token,))
        out = hidden
        for p, j in sorted(order, key=lambda key: key in rest):
            for c, (kept, came) in enumerate(v["piece", p, j]):
                first = (((z_at - p) % pairs) * n_y + (y_at + j) % n_y) * n_core
                first = (first + (core_at + c) % n_core) * o_cols
                branch = kept.astype(jnp.float32) + came.astype(jnp.float32)
                here = lax.dynamic_slice(hidden, (0, first), (tok_rows, o_cols)).astype(jnp.float32)
                out = lax.dynamic_update_slice(out, (here + branch).astype(jnp.bfloat16), (0, first))
        return out

    made = []
    attn = jnp.concatenate(v["attn"], axis=0)
    for k in range(depth):
        for j in range(n_y):
            total = jnp.dot(attn, o_stream.blocks[k, j], preferred_element_type=jnp.float32)
            made.append(total.astype(jnp.bfloat16))
    made = jnp.stack(made, axis=0)[:, None]
    if n_core == 2:
        theirs = swap(made[:, :, tok_rows:], "seq", 1)
        made = jnp.concatenate([made[:, :, :tok_rows], theirs], axis=1)
    made = made.reshape(n_seq, tok_rows, o_cols)
    block = jnp.arange(n_seq, dtype=jnp.int32)
    b_z, b_y, b_c = block // (n_y * n_core), (block // n_core) % n_y, block % n_core
    at = (((z_at - b_z) % depth) * n_y + (b_y - y_at) % n_y) * n_core + (b_c - core_at) % n_core
    whole = jnp.moveaxis(jnp.take(made, at, axis=0), 0, 1).reshape(tok_rows, feat * n_tp)
    branch = lax.psum_scatter(whole, "tp", scatter_dimension=1, tiled=True).astype(jnp.float32)
    return (hidden.astype(jnp.float32) + branch).astype(jnp.bfloat16)


def solution(mesh):
    placed = (
        P("seq", "tp"),
        P("seq", None, None),
        P(),
        P(None, "tp"),
        P("tp", None),
        P(None, "tp"),
        P(None, "tp"),
        P(),
        P("seq", "tp"),
        P("tp", "seq"),
    )
    return jax.shard_map(
        per_device, mesh=mesh, in_specs=placed, out_specs=P("seq", "tp"), check_vma=False
    )
```

time: 429 us -> 223 us (0.52)
  waiting for transfers between devices: 315 us -> 82.3 us
  matrix products: 65.6 us -> 0 us
  Pallas kernels: 0 us -> 63.7 us
  starting transfers between devices: 3.46 us -> 27 us
  local copies, waits for them, and re-layouts: 15.9 us -> 39.3 us
  between operations: 13.3 us -> 0.38 us
  other arithmetic: 15.1 us -> 9.85 us
    all_gather x3 -> x0, waiting for transfers between devices: 216 us -> none  [the longest x1 107 us: per_device(): lax.all_gather(query_weight, 'seq', axis=0, tiled=True)]
    ppermute x1 -> x28, waiting for transfers between devices: 0.93 us -> 82.3 us  [the longest x20 69.1 us: swap(): return lax.ppermute(value, axis, pairs)]
    psum x1 -> x0, waiting for transfers between devices: 67.5 us -> none  [encode(): lax.psum(feed_partial(flat, enc_gain, enc_w1, enc_w2).astype(jnp.bfloat16...]
    dot_general x7 -> x0, matrix products: 65.6 us -> none  [the longest x1 14.6 us: per_device(): jnp.einsum('chmn,cnhd->cmhd', probs, values_all, preferred_element_type=j...]
    pallas_call x0 -> x14, Pallas kernels: none -> 63.7 us  [the longest x3 16.4 us: project(): pl.pallas_call(functools.partial(project_kernel, len(parts)), in_specs=[W...]
    reduce_scatter x1 -> x0, waiting for transfers between devices: 30.1 us -> none  [per_device(): lax.psum_scatter(partial_value.astype(jnp.bfloat16), 'tp', scatter_dimens...]
    ppermute x1 -> x28, starting transfers between devices: 3.12 us -> 27 us  [the longest x20 14.8 us: swap(): return lax.ppermute(value, axis, pairs)]
    unnamed x23 -> x97, local copies, waits for them, and re-layouts: 13 us -> 34.1 us
  transfers between devices with their start and end apart: 6 -> 28, of which waited for: 6 -> 13; matrix products, arithmetic and copies ran while one was open for 18% -> 6% of each run, Pallas kernels for 0% -> 26%
where the time goes in v2:
time: 223 us
  waiting for transfers between devices  82.3 us (37%)
  Pallas kernels  63.7 us (29%)
  local copies, waits for them, and re-layouts  39.3 us (18%)
  starting transfers between devices  27 us (12%)
  other arithmetic  9.85 us (4%)
    ppermute x20, waiting for transfers between devices, swap(): return lax.ppermute(value, axis, pairs)  69.1 us
    unnamed x97, local copies, waits for them, and re-layouts  34.1 us
    pallas_call x3, Pallas kernels, project(): pl.pallas_call(functools.partial(project_kernel, len(parts)), in_specs=[W...  16.4 us
    ppermute x20, starting transfers between devices, swap(): return lax.ppermute(value, axis, pairs)  14.8 us
    pallas_call x4, Pallas kernels, out_products(): pl.pallas_call(functools.partial(out_kernel, len(attns), [[len(b) for b i...  14.3 us
    ppermute x7, waiting for transfers between devices, ring(): lax.ppermute(value, axis, [(i, (i + stride) % count) for i in range(count)])  13.2 us
    pallas_call x3, Pallas kernels, add_query(): pl.pallas_call(functools.partial(query_kernel, len(norms), len(blocks), l...  11.4 us
    pallas_call x2, Pallas kernels, encode_partial(): pl.pallas_call(encode_kernel, in_specs=[WHOLE] * 4, out_specs=WHOLE, out_...  10.5 us
  transfers between devices with their start and end apart: 28, of which 13 were waited for; matrix products, arithmetic and copies ran while one was open for 6% of the time, Pallas kernels for 26%

profile of v2, /device:TPU:0, one launch (start us, length us, event | category | flops | bytes accessed | tf_op | source)
XLA Modules:
  0.0 222.6 jit_solution(6115449284638634391)
XLA Ops:
  0.0 3.0 %collective-permute-start.5 = (bf16[2048,256]{1,0:T(8,128)(2,1)}, bf16[2048,256]{1,0:T(8,128)(2,1)}, u32[]{:S(2)}, u32[]{:S(2)}) collective-permute-start(bf16[2048,256]{1,0:T(8,128)(2,1)} %refs_2_.5), channel_id=1, source_target_pairs={{0,4},{2,6},{4,0},{6,2},{8,12},{10,14},{12,8},{14,10},{16,20},{18,... | collective-permute-start | bytes 3145736 | tf_op jit(solution)/shard_map/out_0_1/ppermute | solution.py:24
  3.0 1.4 constant_dynamic-slice_fusion.1
  4.5 1.6 collective-permute-start
  6.1 2.7 %fusion.20 = (bf16[2,256,896]{2,1,0:T(8,128)(2,1)}, bf16[2,256,896]{2,1,0:T(8,128)(2,1)S(1)}) fusion(bf16[4,256,896]{2,1,0:T(8,128)(2,1)} %param.13), kind=kLoop, calls=%fused_computation.43 | loop fusion | bytes 3670016 | tf_op jit(solution)/shard_map/slice | solution.py:345
  8.9 1.6 collective-permute-start.2
  11.0 2.2 %collective-permute-start.4 = (bf16[512,1024]{1,0:T(8,128)(2,1)S(1)}, bf16[512,1024]{1,0:T(8,128)(2,1)}, u32[]{:S(2)}, u32[]{:S(2)}) collective-permute-start(bf16[512,1024]{1,0:T(8,128)(2,1)S(1)} %pad_maximum_fusion.refs_2_), channel_id=1, source_target_pairs={{0,24},{2,26},{4,28},{6,30},{8,0},{10,2},{12,4},{14,6},{16,8},{18,... | collective-permute-start | bytes 3145736 | tf_op jit(solution)/shard_map/query_3_0/ppermute | solution.py:29
  13.3 5.2 %encode.2.refs_1_ = bf16[512,896]{1,0:T(8,128)(2,1)} custom-call(bf16[512,896]{1,0:T(8,128)(2,1)S(1)} %bitcast.71, f32[1,896]{1,0:T(1,128)S(1)} %reshape.40.gain_ref, bf16[896,1792]{1,0:T(8,128)(2,1)S(1)} %copy-done.38, bf16[1792,896]{1,0:T(8,128)(2,1)S(1)} %copy-done.40), custom_call_target="tpu_custom_call" | custom-call | flops 3288334336 | bytes 6422528 | tf_op jit(solution)/shard_map/encode/encode/pallas_call | solution.py:104
  18.5 8.8 %collective-permute-done.5.refs_2_ = bf16[2048,256]{1,0:T(8,128)(2,1)} collective-permute-done((bf16[2048,256]{1,0:T(8,128)(2,1)}, bf16[2048,256]{1,0:T(8,128)(2,1)}, u32[]{:S(2)}, u32[]{:S(2)}) %collective-permute-start.5) | collective-permute-done | bytes 1048608 | tf_op jit(solution)/shard_map/out_0_1/ppermute | solution.py:24
  27.3 2.0 collective-permute-start.6
  29.3 1.2 copy-done.32
  30.5 1.9 copy-done.39
  32.4 1.9 copy-done.41
  34.3 5.3 %encode.3.refs_1_ = bf16[512,896]{1,0:T(8,128)(2,1)} custom-call(bf16[512,896]{1,0:T(8,128)(2,1)S(1)} %bitcast.69, f32[1,896]{1,0:T(1,128)S(1)} %reshape.40.gain_ref, bf16[896,1792]{1,0:T(8,128)(2,1)S(1)} %copy-done.39, bf16[1792,896]{1,0:T(8,128)(2,1)S(1)} %copy-done.41), custom_call_target="tpu_custom_call" | custom-call | flops 3288334336 | bytes 6422528 | tf_op jit(solution)/shard_map/encode/encode/pallas_call | solution.py:104
  39.6 1.0 copy-done.30
  40.6 9.2 %collective-permute-done.6.refs_2_ = bf16[512,896]{1,0:T(8,128)(2,1)} collective-permute-done((bf16[512,896]{1,0:T(8,128)(2,1)}, bf16[512,896]{1,0:T(8,128)(2,1)}, u32[]{:S(2)}, u32[]{:S(2)}) %collective-permute-start.6) | collective-permute-done | bytes 917536 | tf_op jit(solution)/shard_map/encode_sum/ppermute | solution.py:24
  49.8 8.4 %collective-permute-done.4.refs_5_ = bf16[512,1024]{1,0:T(8,128)(2,1)} collective-permute-done((bf16[512,1024]{1,0:T(8,128)(2,1)S(1)}, bf16[512,1024]{1,0:T(8,128)(2,1)}, u32[]{:S(2)}, u32[]{:S(2)}) %collective-permute-start.4) | collective-permute-done | bytes 1048608 | tf_op jit(solution)/shard_map/query_3_0/ppermute | solution.py:29
  58.2 1.2 copy-done.31
  59.5 1.7 decode.1.refs_0_
  61.2 1.0 collective-permute-start.7
  62.7 1.5 collective-permute-start.10
  65.4 1.3 copy-done
  67.3 2.0 copy-done.16
  69.3 2.0 copy-done.19
  71.4 1.2 copy-done.35
  72.5 6.1 %project.3 = (bf16[512,896]{1,0:T(8,128)(2,1)}, bf16[512,2048]{1,0:T(8,128)(2,1)S(1)}, bf16[512,2048]{1,0:T(8,128)(2,1)S(1)}) custom-call(bf16[512,896]{1,0:T(8,128)(2,1)S(1)} %bitcast.72, bf16[512,896]{1,0:T(8,128)(2,1)} %encode.2.refs_1_, bf16[512,896]{1,0:T(8,128)(2,1)} %collective-permute-done.6.refs_2_, bf16[896,2048]{1,0:T(8,128)(2,1)S(1)} %copy-done.16, ...), custom_call_target="tpu_custom_call" | custom-call | flops 3758096384 | bytes 7340032 | tf_op jit(solution)/shard_map/keys_values/project/pallas_call | solution.py:140
  78.7 5.7 %query.3.refs_5_ = f32[512,1024]{1,0:T(8,128)S(1)} custom-call(s32[8]{0:T(128)S(1)} %stack.88.at_ref, bf16[16,256,256]{2,1,0:T(8,128)(2,1)S(1)} %decode.1.refs_0_, bf16[16,256,256]{2,1,0:T(8,128)(2,1)S(1)} %copy-done.1, bf16[512,1024]{1,0:T(8,128)(2,1)S(1)} %copy-done.15, bf16[512,1024]{1,0:T(8,128)(2,1)} %collective-permute-done.2.refs_3_, ...), custom_call_target="tpu_custom_call" | custom-call | flops 2147483648 | bytes 4194304 | tf_op jit(solution)/shard_map/query_part/query/pallas_call | solution.py:210
  84.5 1.4 copy-done.4
  85.9 24.3 %collective-permute-done.10.refs_4_ = bf16[512,1024]{1,0:T(8,128)(2,1)} collective-permute-done((bf16[512,1024]{1,0:T(8,128)(2,1)}, bf16[512,1024]{1,0:T(8,128)(2,1)}, u32[]{:S(2)}, u32[]{:S(2)}) %collective-permute-start.10) | collective-permute-done | bytes 1048608 | tf_op jit(solution)/shard_map/query_3_1/ppermute | solution.py:24
  110.2 1.2 collective-permute-done.9.refs_4_
  112.4 2.0 copy-done.17
  114.4 2.0 copy-done.20
  116.4 1.2 copy-done.33
  117.6 6.2 %project.4 = (bf16[512,896]{1,0:T(8,128)(2,1)S(1)}, bf16[512,2048]{1,0:T(8,128)(2,1)S(1)}, bf16[512,2048]{1,0:T(8,128)(2,1)S(1)}) custom-call(bf16[512,896]{1,0:T(8,128)(2,1)S(1)} %bitcast.70, bf16[512,896]{1,0:T(8,128)(2,1)} %encode.3.refs_1_, bf16[512,896]{1,0:T(8,128)(2,1)} %collective-permute-done.12.refs_2_, bf16[896,2048]{1,0:T(8,128)(2,1)S(1)} %copy-done.17, ...), custom_call_target="tpu_custom_call" | custom-call | flops 3758096384 | bytes 7340032 | tf_op jit(solution)/shard_map/keys_values/project/pallas_call | solution.py:140
  123.8 1.3 copy-done.26
  126.0 2.1 collective-permute-start.16
  128.0 3.7 %query.4.refs_3_ = f32[512,1024]{1,0:T(8,128)S(1)} custom-call(s32[6]{0:T(128)S(1)} %stack.95.at_ref, bf16[16,256,256]{2,1,0:T(8,128)(2,1)S(1)} %decode.1.refs_0_, bf16[16,256,256]{2,1,0:T(8,128)(2,1)S(1)} %copy-done.2, bf16[512,1024]{1,0:T(8,128)(2,1)} %collective-permute-done.7.refs_2_, bf16[512,1024]{1,0:T(8,128)(2,1)} %collective-permute-done.8.refs_3_, ...), custom_call_target="tpu_custom_call" | custom-call | flops 1610612736 | bytes 3145728 | tf_op jit(solution)/shard_map/query_part/query/pallas_call | solution.py:210
  131.8 4.6 %collective-permute-done.14.refs_2_ = bf16[512,1024]{1,0:T(8,128)(2,1)} collective-permute-done((bf16[512,1024]{1,0:T(8,128)(2,1)}, bf16[512,1024]{1,0:T(8,128)(2,1)}, u32[]{:S(2)}, u32[]{:S(2)}) %collective-permute-start.14) | collective-permute-done | bytes 1048608 | tf_op jit(solution)/shard_map/query_2_1/ppermute | solution.py:24
  136.4 2.4 %collective-permute-done.13.refs_3_ = bf16[2048,256]{1,0:T(8,128)(2,1)} collective-permute-done((bf16[2048,256]{1,0:T(8,128)(2,1)}, bf16[2048,256]{1,0:T(8,128)(2,1)}, u32[]{:S(2)}, u32[]{:S(2)}) %collective-permute-start.13) | collective-permute-done | bytes 1048608 | tf_op jit(solution)/shard_map/out_2_0/ppermute | solution.py:29
  138.8 2.0 query.5
  140.8 1.0 copy-done.12
  141.9 1.2 collective-permute-start.18
  143.1 1.7 collective-permute-start.17
  144.8 2.0 copy-done.18
  146.8 2.0 copy-done.21
  148.9 4.1 %project.5 = (bf16[256,896]{1,0:T(8,128)(2,1)}, bf16[256,2048]{1,0:T(8,128)(2,1)S(1)}, bf16[256,2048]{1,0:T(8,128)(2,1)S(1)}) custom-call(bf16[256,896]{1,0:T(8,128)(2,1)} %collective-permute-done.16.refs_0_, bf16[896,2048]{1,0:T(8,128)(2,1)S(1)} %copy-done.18, bf16[896,2048]{1,0:T(8,128)(2,1)S(1)} %copy-done.21), custom_call_target="tpu_custom_call" | custom-call | flops 1879048192 | bytes 7340032 | tf_op jit(solution)/shard_map/keys_values_earlier/project/pallas_call | solution.py:140
  153.4 1.1 copy-done.23
  155.2 9.5 %attend.1 = bf16[320,2048]{1,0:T(8,128)(2,1)S(1)} custom-call(bf16[320,2048]{1,0:T(8,128)(2,1)S(1)} %fusion.3.q_ref, bf16[256,2048]{1,0:T(8,128)(2,1)S(1)} %get-tuple-element.89.refs_0_, bf16[512,2048]{1,0:T(8,128)(2,1)S(1)} %copy-done.23, bf16[512,2048]{1,0:T(8,128)(2,1)S(1)} %copy-done.27, bf16[256,2048]{1,0:T(8,128)(2,1)S(1)} %get-tuple-element.90.refs_3_, ...), custom_call_target="tpu_custom_call" | custom-call | bytes 1024 | tf_op jit(solution)/shard_map/attention/attend/pallas_call | solution.py:294
  165.1 2.5 %collective-permute-done.18.refs_4_ = bf16[2048,256]{1,0:T(8,128)(2,1)S(1)} collective-permute-done((bf16[2048,256]{1,0:T(8,128)(2,1)}, bf16[2048,256]{1,0:T(8,128)(2,1)S(1)}, u32[]{:S(2)}, u32[]{:S(2)}) %collective-permute-start.18) | collective-permute-done | bytes 1048608 | tf_op jit(solution)/shard_map/out_1_1/ppermute | solution.py:24
  168.6 1.0 copy-done.9
  169.6 1.2 collective-permute-start.24
  170.8 2.8 %collective-permute-start.23 = (bf16[2048,256]{1,0:T(8,128)(2,1)}, bf16[2048,256]{1,0:T(8,128)(2,1)}, u32[]{:S(2)}, u32[]{:S(2)}) collective-permute-start(bf16[2048,256]{1,0:T(8,128)(2,1)} %collective-permute-done.5.refs_2_), channel_id=1, source_target_pairs={{0,24},{2,26},{4,28},{6,30},{8,0},{10,2},{12,4},{14,6},{16,8},{18,... | collective-permute-start | bytes 3145736 | tf_op jit(solution)/shard_map/out_3_1/ppermute | solution.py:29
  173.7 1.2 copy-done.10
  174.9 3.4 %out.4 = (bf16[2,256,256]{2,1,0:T(8,128)(2,1)S(1)}, bf16[2,256,256]{2,1,0:T(8,128)(2,1)S(1)}) custom-call(s32[2]{0:T(128)S(1)} %get-tuple-element.113.near_ref, bf16[256,2048]{1,0:T(8,128)(2,1)S(1)} %slice_select_fusion.refs_0_, bf16[256,2048]{1,0:T(8,128)(2,1)S(1)} %collective-permute-done.19.refs_1_, bf16[2048,256]{1,0:T(8,128)(2,1)} %refs_2_.5, ...), custom_call_target="tpu_custom_call" | custom-call | bytes 1024 | tf_op jit(solution)/shard_map/scatter/out/pallas_call | solution.py:249
  178.3 1.5 collective-permute-done.20
  180.5 3.4 %out.5 = (bf16[2,256,256]{2,1,0:T(8,128)(2,1)S(1)}, bf16[2,256,256]{2,1,0:T(8,128)(2,1)S(1)}) custom-call(s32[2]{0:T(128)S(1)} %get-tuple-element.114.near_ref, bf16[256,2048]{1,0:T(8,128)(2,1)S(1)} %slice_select_fusion.refs_0_, bf16[256,2048]{1,0:T(8,128)(2,1)S(1)} %collective-permute-done.19.refs_1_, bf16[2048,256]{1,0:T(8,128)(2,1)} %refs_2_.5, ...), custom_call_target="tpu_custom_call" | custom-call | bytes 1024 | tf_op jit(solution)/shard_map/scatter/out/pallas_call | solution.py:249
  184.0 10.6 %collective-permute-done.24.refs_3_ = bf16[2048,256]{1,0:T(8,128)(2,1)} collective-permute-done((bf16[2048,256]{1,0:T(8,128)(2,1)}, bf16[2048,256]{1,0:T(8,128)(2,1)}, u32[]{:S(2)}, u32[]{:S(2)}) %collective-permute-start.24) | collective-permute-done | bytes 1048608 | tf_op jit(solution)/shard_map/out_2_1/ppermute | solution.py:24
  194.6 1.2 collective-permute-done.23.refs_5_
  196.6 4.2 %out.6 = (bf16[2,256,256]{2,1,0:T(8,128)(2,1)S(1)}, bf16[2,256,256]{2,1,0:T(8,128)(2,1)}) custom-call(s32[2]{0:T(128)S(1)} %get-tuple-element.113.near_ref, bf16[256,2048]{1,0:T(8,128)(2,1)S(1)} %slice_select_fusion.refs_0_, bf16[256,2048]{1,0:T(8,128)(2,1)S(1)} %collective-permute-done.19.refs_1_, bf16[2048,256]{1,0:T(8,128)(2,1)} %collective-permute-done.5.refs_2_, ...), custom_call_target="tpu_custom_call" | custom-call | bytes 1024 | tf_op jit(solution)/shard_map/scatter/out/pallas_call | solution.py:249
  201.4 1.0 copy.13
  202.4 1.8 fusion.12
  204.2 1.1 pad_maximum_fusion.2
  205.9 1.7 fusion.13
  208.3 3.3 %out.7 = (bf16[2,256,256]{2,1,0:T(8,128)(2,1)S(1)}, bf16[2,256,256]{2,1,0:T(8,128)(2,1)S(1)}) custom-call(s32[2]{0:T(128)S(1)} %get-tuple-element.114.near_ref, bf16[256,2048]{1,0:T(8,128)(2,1)S(1)} %slice_select_fusion.refs_0_, bf16[256,2048]{1,0:T(8,128)(2,1)S(1)} %collective-permute-done.19.refs_1_, bf16[2048,256]{1,0:T(8,128)(2,1)} %collective-permute-done.5.refs_2_, ...), custom_call_target="tpu_custom_call" | custom-call | bytes 1024 | tf_op jit(solution)/shard_map/scatter/out/pallas_call | solution.py:249
  212.6 7.1 %collective-permute-done.26 = bf16[4,256,256]{2,1,0:T(8,128)(2,1)S(1)} collective-permute-done((bf16[4,256,256]{2,1,0:T(8,128)(2,1)S(1)}, bf16[4,256,256]{2,1,0:T(8,128)(2,1)S(1)}, u32[]{:S(2)}, u32[]{:S(2)}) %collective-permute-start.26) | collective-permute-done | bytes 524320 | tf_op jit(solution)/shard_map/scatter/ppermute | solution.py:24
  (128 shorter events, 15.0 us)
Async XLA Ops:
  0.0 4.5 %copy-start.3 = (bf16[256,2048]{1,0:T(8,128)(2,1)S(1)}, bf16[256,2048]{1,0:T(8,128)(2,1)}, u32[]{:S(2)}) copy-start(bf16[256,2048]{1,0:T(8,128)(2,1)} %own_ref.1) | copy-start | bytes 3145732
  0.0 6.0 %copy-start.46 = (f32[896]{0:T(1024)S(1)}, f32[896]{0:T(1024)}, u32[]{:S(2)}) copy-start(f32[896]{0:T(1024)} %param.14) | copy-start | bytes 10756
  0.0 27.3 %collective-permute-start.5 = (bf16[2048,256]{1,0:T(8,128)(2,1)}, bf16[2048,256]{1,0:T(8,128)(2,1)}, u32[]{:S(2)}, u32[]{:S(2)}) collective-permute-start(bf16[2048,256]{1,0:T(8,128)(2,1)} %refs_2_.5), channel_id=1, source_target_pairs={{0,4},{2,6},{4,0},{6,2},{8,12},{10,14},{12,8},{14,10},{16,20},{18,... | collective-permute-start | bytes 3145736 | tf_op jit(solution)/shard_map/out_0_1/ppermute | solution.py:24
  3.0 10.3 %copy-start.40 = (bf16[1792,896]{1,0:T(8,128)(2,1)S(1)}, bf16[1792,896]{1,0:T(8,128)(2,1)}, u32[]{:S(2)}) copy-start(bf16[1792,896]{1,0:T(8,128)(2,1)} %second_ref.3) | copy-start | bytes 9633796
  4.4 4.4 %collective-permute-start.1 = (bf16[256,1024]{1,0:T(8,128)(2,1)S(1)}, bf16[256,1024]{1,0:T(8,128)(2,1)S(1)}, u32[]{:S(2)}, u32[]{:S(2)}) collective-permute-start(bf16[256,1024]{1,0:T(8,128)(2,1)S(1)} %get-tuple-element.120), channel_id=1, source_target_pairs={{0,2},{2,0},{4,6},{6,4},{8,10},{10,8},{12,14},{14,12},{16,18},{18,... | collective-permute-start | bytes 1572872 | tf_op jit(solution)/shard_map/ppermute | solution.py:24
  4.5 35.1 %collective-permute-start = (bf16[256,2048]{1,0:T(8,128)(2,1)S(1)}, bf16[256,2048]{1,0:T(8,128)(2,1)S(1)}, u32[]{:S(2)}, u32[]{:S(2)}) collective-permute-start(bf16[256,2048]{1,0:T(8,128)(2,1)S(1)} %copy-done.3), channel_id=1, source_target_pairs={{0,1},{1,0},{2,3},{3,2},{4,5},{5,4},{6,7},{7,6},{8,9},{9,8},{10,11... | collective-permute-start | bytes 3145736 | tf_op jit(solution)/shard_map/ppermute | solution.py:24
  6.0 7.2 %copy-start.38 = (bf16[896,1792]{1,0:T(8,128)(2,1)S(1)}, bf16[896,1792]{1,0:T(8,128)(2,1)}, u32[]{:S(2)}) copy-start(bf16[896,1792]{1,0:T(8,128)(2,1)} %first_ref.3) | copy-start | bytes 9633796
  8.8 9.7 %copy-start.34 = (bf16[2,256,896]{2,1,0:T(8,128)(2,1)}, bf16[2,256,896]{2,1,0:T(8,128)(2,1)S(1)}, u32[]{:S(2)}) copy-start(bf16[2,256,896]{2,1,0:T(8,128)(2,1)S(1)} %get-tuple-element.116) | copy-start | bytes 2752516
  8.8 9.7 %copy-start.14 = (bf16[512,1024]{1,0:T(8,128)(2,1)}, bf16[512,1024]{1,0:T(8,128)(2,1)S(1)}, u32[]{:S(2)}) copy-start(bf16[512,1024]{1,0:T(8,128)(2,1)S(1)} %pad_maximum_fusion.refs_2_) | copy-start | bytes 3145732
  8.9 41.0 %collective-permute-start.2 = (bf16[512,1024]{1,0:T(8,128)(2,1)S(1)}, bf16[512,1024]{1,0:T(8,128)(2,1)}, u32[]{:S(2)}, u32[]{:S(2)}) collective-permute-start(bf16[512,1024]{1,0:T(8,128)(2,1)S(1)} %pad_maximum_fusion.refs_2_), channel_id=1, source_target_pairs={{0,8},{2,10},{4,12},{6,14},{8,16},{10,18},{12,20},{14,22},{16,24},... | collective-permute-start | bytes 3145736 | tf_op jit(solution)/shard_map/query_1_0/ppermute | solution.py:29
  10.5 39.3 %collective-permute-start.3 = (bf16[512,1024]{1,0:T(8,128)(2,1)S(1)}, bf16[512,1024]{1,0:T(8,128)(2,1)}, u32[]{:S(2)}, u32[]{:S(2)}) collective-permute-start(bf16[512,1024]{1,0:T(8,128)(2,1)S(1)} %pad_maximum_fusion.refs_2_), channel_id=1, source_target_pairs={{0,4},{2,6},{4,0},{6,2},{8,12},{10,14},{12,8},{14,10},{16,20},{18,... | collective-permute-start | bytes 3145736 | tf_op jit(solution)/shard_map/query_0_1/ppermute | solution.py:24
  11.0 47.2 %collective-permute-start.4 = (bf16[512,1024]{1,0:T(8,128)(2,1)S(1)}, bf16[512,1024]{1,0:T(8,128)(2,1)}, u32[]{:S(2)}, u32[]{:S(2)}) collective-permute-start(bf16[512,1024]{1,0:T(8,128)(2,1)S(1)} %pad_maximum_fusion.refs_2_), channel_id=1, source_target_pairs={{0,24},{2,26},{4,28},{6,30},{8,0},{10,2},{12,4},{14,6},{16,8},{18,... | collective-permute-start | bytes 3145736 | tf_op jit(solution)/shard_map/query_3_0/ppermute | solution.py:29
  13.2 16.1 %copy-start.47 = (s32[2]{0:T(128)S(1)}, s32[2]{0:T(128)}, u32[]{:S(2)}) copy-start(s32[2]{0:T(128)} %constant.268.clone) | copy-start | bytes 28
  27.3 22.5 %collective-permute-start.6 = (bf16[512,896]{1,0:T(8,128)(2,1)}, bf16[512,896]{1,0:T(8,128)(2,1)}, u32[]{:S(2)}, u32[]{:S(2)}) collective-permute-start(bf16[512,896]{1,0:T(8,128)(2,1)} %encode.2.refs_1_), channel_id=1, source_target_pairs={{0,1},{1,0},{2,3},{3,2},{4,5},{5,4},{6,7},{7,6},{8,9},{9,8},{10,11... | collective-permute-start | bytes 2752520 | tf_op jit(solution)/shard_map/encode_sum/ppermute | solution.py:24
  30.5 1.9 copy-start.39
  32.4 1.9 copy-start.41
  34.3 23.9 %copy-start.37 = (f32[4096]{0:T(1024)S(1)}, f32[4096]{0:T(1024)}, u32[]{:S(2)}) copy-start(f32[4096]{0:T(1024)} %param.19) | copy-start | bytes 49156
  61.1 4.2 %collective-permute-start.11 = (bf16[16,256,256]{2,1,0:T(8,128)(2,1)S(1)}, bf16[16,256,256]{2,1,0:T(8,128)(2,1)S(1)}, u32[]{:S(2)}, u32[]{:S(2)}) collective-permute-start(bf16[16,256,256]{2,1,0:T(8,128)(2,1)S(1)} %decode.1.refs_0_), channel_id=1, source_target_pairs={{0,2},{2,0},{4,6},{6,4},{8,10},{10,8},{12,14},{14,12},{16,18},{18,... | collective-permute-start | bytes 6291464 | tf_op jit(solution)/shard_map/decode/ppermute | solution.py:24
  61.2 49.0 %collective-permute-start.7 = (bf16[512,1024]{1,0:T(8,128)(2,1)}, bf16[512,1024]{1,0:T(8,128)(2,1)}, u32[]{:S(2)}, u32[]{:S(2)}) collective-permute-start(bf16[512,1024]{1,0:T(8,128)(2,1)} %collective-permute-done.2.refs_3_), channel_id=1, source_target_pairs={{0,8},{2,10},{4,12},{6,14},{8,16},{10,18},{12,20},{14,22},{16,24},... | collective-permute-start | bytes 3145736 | tf_op jit(solution)/shard_map/query_2_0/ppermute | solution.py:29
  62.2 48.0 %collective-permute-start.8 = (bf16[512,1024]{1,0:T(8,128)(2,1)}, bf16[512,1024]{1,0:T(8,128)(2,1)}, u32[]{:S(2)}, u32[]{:S(2)}) collective-permute-start(bf16[512,1024]{1,0:T(8,128)(2,1)} %collective-permute-done.2.refs_3_), channel_id=1, source_target_pairs={{0,4},{2,6},{4,0},{6,2},{8,12},{10,14},{12,8},{14,10},{16,20},{18,... | collective-permute-start | bytes 3145736 | tf_op jit(solution)/shard_map/query_1_1/ppermute | solution.py:24
  62.7 47.5 %collective-permute-start.10 = (bf16[512,1024]{1,0:T(8,128)(2,1)}, bf16[512,1024]{1,0:T(8,128)(2,1)}, u32[]{:S(2)}, u32[]{:S(2)}) collective-permute-start(bf16[512,1024]{1,0:T(8,128)(2,1)} %collective-permute-done.4.refs_5_), channel_id=1, source_target_pairs={{0,4},{2,6},{4,0},{6,2},{8,12},{10,14},{12,8},{14,10},{16,20},{18,... | collective-permute-start | bytes 3145736 | tf_op jit(solution)/shard_map/query_3_1/ppermute | solution.py:24
  64.2 47.1 %collective-permute-start.9 = (bf16[2048,256]{1,0:T(8,128)(2,1)}, bf16[2048,256]{1,0:T(8,128)(2,1)}, u32[]{:S(2)}, u32[]{:S(2)}) collective-permute-start(bf16[2048,256]{1,0:T(8,128)(2,1)} %refs_2_.5), channel_id=1, source_target_pairs={{0,8},{2,10},{4,12},{6,14},{8,16},{10,18},{12,20},{14,22},{16,24},... | collective-permute-start | bytes 3145736 | tf_op jit(solution)/shard_map/out_1_0/ppermute | solution.py:29
  65.4 1.3 copy-start
  66.7 44.7 %collective-permute-start.12 = (bf16[512,896]{1,0:T(8,128)(2,1)}, bf16[512,896]{1,0:T(8,128)(2,1)}, u32[]{:S(2)}, u32[]{:S(2)}) collective-permute-start(bf16[512,896]{1,0:T(8,128)(2,1)} %encode.3.refs_1_), channel_id=1, source_target_pairs={{0,1},{1,0},{2,3},{3,2},{4,5},{5,4},{6,7},{7,6},{8,9},{9,8},{10,11... | collective-permute-start | bytes 2752520 | tf_op jit(solution)/shard_map/encode_sum/ppermute | solution.py:24
  67.3 2.0 copy-start.16
  69.3 2.0 copy-start.19
  72.5 6.2 %copy-start.1 = (bf16[16,256,256]{2,1,0:T(8,128)(2,1)S(1)}, bf16[16,256,256]{2,1,0:T(8,128)(2,1)}, u32[]{:S(2)}) copy-start(bf16[16,256,256]{2,1,0:T(8,128)(2,1)} %copy-done) | copy-start | bytes 6291460
  72.5 6.2 %copy-start.15 = (bf16[512,1024]{1,0:T(8,128)(2,1)S(1)}, bf16[512,1024]{1,0:T(8,128)(2,1)}, u32[]{:S(2)}) copy-start(bf16[512,1024]{1,0:T(8,128)(2,1)} %copy-done.14) | copy-start | bytes 3145732
  78.7 5.7 %copy-start.22 = (bf16[512,2048]{1,0:T(8,128)(2,1)}, bf16[512,2048]{1,0:T(8,128)(2,1)S(1)}, u32[]{:S(2)}) copy-start(bf16[512,2048]{1,0:T(8,128)(2,1)S(1)} %get-tuple-element.70.refs_1_) | copy-start | bytes 6291460
  78.7 5.7 %copy-start.24 = (bf16[512,2048]{1,0:T(8,128)(2,1)}, bf16[512,2048]{1,0:T(8,128)(2,1)S(1)}, u32[]{:S(2)}) copy-start(bf16[512,2048]{1,0:T(8,128)(2,1)S(1)} %get-tuple-element.71.refs_4_) | copy-start | bytes 6291460
  84.5 1.4 copy-start.4
  111.4 25.0 %collective-permute-start.14 = (bf16[512,1024]{1,0:T(8,128)(2,1)}, bf16[512,1024]{1,0:T(8,128)(2,1)}, u32[]{:S(2)}, u32[]{:S(2)}) collective-permute-start(bf16[512,1024]{1,0:T(8,128)(2,1)} %collective-permute-done.7.refs_2_), channel_id=1, source_target_pairs={{0,4},{2,6},{4,0},{6,2},{8,12},{10,14},{12,8},{14,10},{16,20},{18,... | collective-permute-start | bytes 3145736 | tf_op jit(solution)/shard_map/query_2_1/ppermute | solution.py:24
  112.2 26.6 %collective-permute-start.13 = (bf16[2048,256]{1,0:T(8,128)(2,1)}, bf16[2048,256]{1,0:T(8,128)(2,1)}, u32[]{:S(2)}, u32[]{:S(2)}) collective-permute-start(bf16[2048,256]{1,0:T(8,128)(2,1)} %collective-permute-done.9.refs_4_), channel_id=1, source_target_pairs={{0,8},{2,10},{4,12},{6,14},{8,16},{10,18},{12,20},{14,22},{16,24},... | collective-permute-start | bytes 3145736 | tf_op jit(solution)/shard_map/out_2_0/ppermute | solution.py:29
  112.4 2.0 copy-start.17
  114.4 2.0 copy-start.20
  117.6 10.4 %copy-start.2 = (bf16[16,256,256]{2,1,0:T(8,128)(2,1)S(1)}, bf16[16,256,256]{2,1,0:T(8,128)(2,1)}, u32[]{:S(2)}) copy-start(bf16[16,256,256]{2,1,0:T(8,128)(2,1)} %copy-done) | copy-start | bytes 6291460
  117.6 10.4 %copy-start.5 = (f32[512,1024]{1,0:T(8,128)S(1)}, f32[512,1024]{1,0:T(8,128)}, u32[]{:S(2)}) copy-start(f32[512,1024]{1,0:T(8,128)} %copy-done.4) | copy-start | bytes 6291460
  125.1 6.7 %copy-start.28 = (bf16[512,2048]{1,0:T(8,128)(2,1)}, bf16[512,2048]{1,0:T(8,128)(2,1)S(1)}, u32[]{:S(2)}) copy-start(bf16[512,2048]{1,0:T(8,128)(2,1)S(1)} %get-tuple-element.81.refs_5_) | copy-start | bytes 6291460
  126.0 17.2 %collective-permute-start.16 = (bf16[256,896]{1,0:T(8,128)(2,1)}, bf16[256,896]{1,0:T(8,128)(2,1)}, u32[]{:S(2)}, u32[]{:S(2)}) collective-permute-start(bf16[256,896]{1,0:T(8,128)(2,1)} %slice.78), channel_id=1, source_target_pairs={{0,2},{2,4},{4,6},{6,8},{8,10},{10,12},{12,14},{14,16},{16,18},{18... | collective-permute-start | bytes 1376264 | tf_op jit(solution)/shard_map/keys_values/ppermute | solution.py:381
  141.8 11.2 %collective-permute-start.15 = (bf16[256,1024]{1,0:T(8,128)(2,1)S(1)}, bf16[256,1024]{1,0:T(8,128)(2,1)S(1)}, u32[]{:S(2)}, u32[]{:S(2)}) collective-permute-start(bf16[256,1024]{1,0:T(8,128)(2,1)S(1)} %slice.97), channel_id=1, source_target_pairs={{0,2},{2,0},{4,6},{6,4},{8,10},{10,8},{12,14},{14,12},{16,18},{18,... | collective-permute-start | bytes 1572872 | tf_op jit(solution)/shard_map/attention/ppermute | solution.py:24
  141.9 11.1 %copy-start.13 = (bf16[512,1024]{1,0:T(8,128)(2,1)S(1)}, bf16[512,1024]{1,0:T(8,128)(2,1)}, u32[]{:S(2)}) copy-start(bf16[512,1024]{1,0:T(8,128)(2,1)} %copy-done.12) | copy-start | bytes 3145732
  141.9 25.8 %collective-permute-start.18 = (bf16[2048,256]{1,0:T(8,128)(2,1)}, bf16[2048,256]{1,0:T(8,128)(2,1)S(1)}, u32[]{:S(2)}, u32[]{:S(2)}) collective-permute-start(bf16[2048,256]{1,0:T(8,128)(2,1)} %collective-permute-done.9.refs_4_), channel_id=1, source_target_pairs={{0,4},{2,6},{4,0},{6,2},{8,12},{10,14},{12,8},{14,10},{16,20},{18,... | collective-permute-start | bytes 3145736 | tf_op jit(solution)/shard_map/out_1_1/ppermute | solution.py:24
  143.1 25.5 %collective-permute-start.17 = (bf16[2048,256]{1,0:T(8,128)(2,1)}, bf16[2048,256]{1,0:T(8,128)(2,1)S(1)}, u32[]{:S(2)}, u32[]{:S(2)}) collective-permute-start(bf16[2048,256]{1,0:T(8,128)(2,1)} %refs_2_.5), channel_id=1, source_target_pairs={{0,24},{2,26},{4,28},{6,30},{8,0},{10,2},{12,4},{14,6},{16,8},{18,... | collective-permute-start | bytes 3145736 | tf_op jit(solution)/shard_map/out_3_0/ppermute | solution.py:29
  144.8 2.0 copy-start.18
  146.8 2.0 copy-start.21
  148.9 4.5 %copy-start.27 = (bf16[512,2048]{1,0:T(8,128)(2,1)S(1)}, bf16[512,2048]{1,0:T(8,128)(2,1)}, u32[]{:S(2)}) copy-start(bf16[512,2048]{1,0:T(8,128)(2,1)} %copy-done.26) | copy-start | bytes 6291460
  148.9 4.5 %copy-start.29 = (bf16[512,2048]{1,0:T(8,128)(2,1)S(1)}, bf16[512,2048]{1,0:T(8,128)(2,1)}, u32[]{:S(2)}) copy-start(bf16[512,2048]{1,0:T(8,128)(2,1)} %copy-done.28) | copy-start | bytes 6291460
  153.0 1.6 copy-start.23
  153.0 2.2 copy-start.25
  165.0 8.6 %collective-permute-start.19 = (bf16[256,2048]{1,0:T(8,128)(2,1)S(1)}, bf16[256,2048]{1,0:T(8,128)(2,1)S(1)}, u32[]{:S(2)}, u32[]{:S(2)}) collective-permute-start(bf16[256,2048]{1,0:T(8,128)(2,1)S(1)} %slice_select_fusion.refs_0_), channel_id=1, source_target_pairs={{0,2},{2,0},{4,6},{6,4},{8,10},{10,8},{12,14},{14,12},{16,18},{18,... | collective-permute-start | bytes 3145736 | tf_op jit(solution)/shard_map/attention/ppermute | solution.py:24
  169.6 25.0 %collective-permute-start.24 = (bf16[2048,256]{1,0:T(8,128)(2,1)}, bf16[2048,256]{1,0:T(8,128)(2,1)}, u32[]{:S(2)}, u32[]{:S(2)}) collective-permute-start(bf16[2048,256]{1,0:T(8,128)(2,1)} %collective-permute-done.13.refs_3_), channel_id=1, source_target_pairs={{0,4},{2,6},{4,0},{6,2},{8,12},{10,14},{12,8},{14,10},{16,20},{18,... | collective-permute-start | bytes 3145736 | tf_op jit(solution)/shard_map/out_2_1/ppermute | solution.py:24
  170.8 25.1 %collective-permute-start.23 = (bf16[2048,256]{1,0:T(8,128)(2,1)}, bf16[2048,256]{1,0:T(8,128)(2,1)}, u32[]{:S(2)}, u32[]{:S(2)}) collective-permute-start(bf16[2048,256]{1,0:T(8,128)(2,1)} %collective-permute-done.5.refs_2_), channel_id=1, source_target_pairs={{0,24},{2,26},{4,28},{6,30},{8,0},{10,2},{12,4},{14,6},{16,8},{18,... | collective-permute-start | bytes 3145736 | tf_op jit(solution)/shard_map/out_3_1/ppermute | solution.py:29
  174.9 5.7 %copy-start.11 = (bf16[2048,256]{1,0:T(8,128)(2,1)S(1)}, bf16[2048,256]{1,0:T(8,128)(2,1)}, u32[]{:S(2)}) copy-start(bf16[2048,256]{1,0:T(8,128)(2,1)} %copy-done.9) | copy-start | bytes 3145732
  178.3 1.6 collective-permute-start.20
  179.9 15.9 %collective-permute-start.21 = (bf16[4,256,256]{2,1,0:T(8,128)(2,1)S(1)}, bf16[4,256,256]{2,1,0:T(8,128)(2,1)S(1)}, u32[]{:S(2)}, u32[]{:S(2)}) collective-permute-start(bf16[4,256,256]{2,1,0:T(8,128)(2,1)S(1)} %pad_maximum_fusion.1), channel_id=1, source_target_pairs={{0,1},{1,0},{2,3},{3,2},{4,5},{5,4},{6,7},{7,6},{8,9},{9,8},{10,11... | collective-permute-start | bytes 1572872 | tf_op jit(solution)/shard_map/scatter/ppermute | solution.py:24
  180.5 16.0 %copy-start.7 = (bf16[2048,256]{1,0:T(8,128)(2,1)S(1)}, bf16[2048,256]{1,0:T(8,128)(2,1)}, u32[]{:S(2)}) copy-start(bf16[2048,256]{1,0:T(8,128)(2,1)} %copy-done.6) | copy-start | bytes 3145732
  183.9 11.9 %collective-permute-start.22 = (bf16[2,256,256]{2,1,0:T(8,128)(2,1)S(1)}, bf16[2,256,256]{2,1,0:T(8,128)(2,1)S(1)}, u32[]{:S(2)}, u32[]{:S(2)}) collective-permute-start(bf16[2,256,256]{2,1,0:T(8,128)(2,1)S(1)} %get-tuple-element.101), channel_id=1, source_target_pairs={{0,2},{2,0},{4,6},{6,4},{8,10},{10,8},{12,14},{14,12},{16,18},{18,... | collective-permute-start | bytes 786440 | tf_op jit(solution)/shard_map/scatter/ppermute | solution.py:24
  196.5 4.2 %copy-start.42 = (bf16[4,256,256]{2,1,0:T(8,128)(2,1)}, bf16[4,256,256]{2,1,0:T(8,128)(2,1)S(1)}, u32[]{:S(2)}) copy-start(bf16[4,256,256]{2,1,0:T(8,128)(2,1)S(1)} %collective-permute-done.21) | copy-start | bytes 1572868
  201.4 2.8 %collective-permute-start.25 = (bf16[2,256,256]{2,1,0:T(8,128)(2,1)}, bf16[2,256,256]{2,1,0:T(8,128)(2,1)}, u32[]{:S(2)}, u32[]{:S(2)}) collective-permute-start(bf16[2,256,256]{2,1,0:T(8,128)(2,1)} %get-tuple-element.108), channel_id=1, source_target_pairs={{0,2},{2,0},{4,6},{6,4},{8,10},{10,8},{12,14},{14,12},{16,18},{18,... | collective-permute-start | bytes 786440 | tf_op jit(solution)/shard_map/scatter/ppermute | solution.py:24
  202.4 5.2 %copy-start.43 = (bf16[4,256,256]{2,1,0:T(8,128)(2,1)S(1)}, bf16[4,256,256]{2,1,0:T(8,128)(2,1)}, u32[]{:S(2)}) copy-start(bf16[4,256,256]{2,1,0:T(8,128)(2,1)} %copy-done.42) | copy-start | bytes 1572868
  202.4 5.9 %copy-start.8 = (bf16[2048,256]{1,0:T(8,128)(2,1)S(1)}, bf16[2048,256]{1,0:T(8,128)(2,1)}, u32[]{:S(2)}) copy-start(bf16[2048,256]{1,0:T(8,128)(2,1)} %copy-done.6) | copy-start | bytes 3145732
  205.3 14.4 %collective-permute-start.26 = (bf16[4,256,256]{2,1,0:T(8,128)(2,1)S(1)}, bf16[4,256,256]{2,1,0:T(8,128)(2,1)S(1)}, u32[]{:S(2)}, u32[]{:S(2)}) collective-permute-start(bf16[4,256,256]{2,1,0:T(8,128)(2,1)S(1)} %pad_maximum_fusion.2), channel_id=1, source_target_pairs={{0,1},{1,0},{2,3},{3,2},{4,5},{5,4},{6,7},{7,6},{8,9},{9,8},{10,11... | collective-permute-start | bytes 1572872 | tf_op jit(solution)/shard_map/scatter/ppermute | solution.py:24
  208.3 3.6 %copy-start.45 = (bf16[2,256,256]{2,1,0:T(8,128)(2,1)S(1)}, bf16[2,256,256]{2,1,0:T(8,128)(2,1)}, u32[]{:S(2)}) copy-start(bf16[2,256,256]{2,1,0:T(8,128)(2,1)} %copy-done.44) | copy-start | bytes 786436
  211.6 8.8 %collective-permute-start.27 = (bf16[2,256,256]{2,1,0:T(8,128)(2,1)S(1)}, bf16[2,256,256]{2,1,0:T(8,128)(2,1)S(1)}, u32[]{:S(2)}, u32[]{:S(2)}) collective-permute-start(bf16[2,256,256]{2,1,0:T(8,128)(2,1)S(1)} %get-tuple-element.112), channel_id=1, source_target_pairs={{0,2},{2,0},{4,6},{6,4},{8,10},{10,8},{12,14},{14,12},{16,18},{18,... | collective-permute-start | bytes 786440 | tf_op jit(solution)/shard_map/scatter/ppermute | solution.py:24
  (12 other events, 12.6 us)

commit v3 on v2

--- a/solution.py
+++ b/solution.py
@@ -420,25 +420,43 @@
 
     pairs = depth // 2
 
-    @named("scatter")
-    def scatter(keys, mark):
+    def out_part(keys, away, mark):
         stay = jnp.stack(
             [(((z_at - p) % depth) // pairs == tp_at).astype(jnp.int32) for p, j in keys]
         )
         attns = tuple(after(a, *mark) for a in v["attn"])
         blocks = [((o_stream.blocks[p, j],), (o_stream.blocks[p + pairs, j],)) for p, j in keys]
-        sent = out_products(1 - stay, attns, blocks)
-        if n_core == 2:
-            sent = (sent[0], swap(sent[1], "seq", 1))
-        kept = out_products(stay, tuple(after(a, *sent) for a in attns), blocks)
-        if n_core == 2:
-            kept = (kept[0], swap(kept[1], "seq", 1))
+        made = out_products(1 - stay if away else stay, attns, blocks)
+        return (made[0], swap(made[1], "seq", 1)) if n_core == 2 else made
+
+    @named("send")
+    def send(keys, mark):
+        sent = out_part(keys, True, mark)
         came = swap(jnp.concatenate(sent, axis=0), "tp", 1)
         for i, key in enumerate(keys):
-            v[("piece",) + key] = [
-                (kept[c][i], came[c * len(keys) + i]) for c in range(n_core)
+            v[("came",) + key] = [came[c * len(keys) + i] for c in range(n_core)]
+        return (came,), tuple(sent)
+
+    @named("keep")
+    def keep(keys, mark):
+        kept = out_part(keys, False, mark)
+        for i, key in enumerate(keys):
+            v[("piece",) + key] = [(kept[c][i], v[("came",) + key][c]) for c in range(n_core)]
+        return tuple(kept)
+
+    v["mixed"] = hidden
+
+    def place(keys):
+        for p, j in keys:
+            first = (((z_at - p) % pairs) * n_y + (y_at + j) % n_y) * n_core * o_cols
+            sums = [
+                kept.astype(jnp.float32) + came.astype(jnp.float32) for kept, came in v["piece", p, j]
             ]
-        return (came,) + tuple(kept)
+            branch = ordered(core_first, *sums, 1) if n_core == 2 else sums[0]
+            here = lax.dynamic_slice(hidden, (0, first), branch.shape).astype(jnp.float32)
+            v["mixed"] = lax.dynamic_update_slice(
+                v["mixed"], (here + branch).astype(jnp.bfloat16), (0, first)
+            )
 
     scatters = n_tp == 2 and depth % 4 == 0
     q, o = q_stream, o_stream
@@ -447,8 +465,8 @@
             [(q, 1, 0, "on"), (q, 0, 1, "y"), (q, 3, 0, "back"), (o, 0, 1, "y")],
             [(q, 2, 0, "on"), (q, 1, 1, "y"), (o, 1, 0, "on"), (q, 3, 1, "y")],
             [(o, 2, 0, "on"), (q, 2, 1, "y")],
-            [(o, 3, 0, "back"), (o, 1, 1, "y")],
-            [(o, 3, 1, "back"), (o, 2, 1, "y")],
+            [(o, 3, 0, "back"), (o, 2, 1, "y")],
+            [(o, 3, 1, "back"), (o, 1, 1, "y")],
         ]
     else:
         plan = []
@@ -487,26 +505,31 @@
                 for key in keys
                 if key not in made and {(o,) + key, (o, key[0] + pairs, key[1])} <= set(arrived)
             ]
+            first = ()
+            for j in range(n_y):
+                here = [key for key in keys if key[1] == j]
+                if here:
+                    made.update(here)
+                    came, _ = send(here, mark)
+                    values += came
+                    first = first or came
             if keys:
-                made.update(keys)
-                values += scatter(keys, mark)
+                keep(keys, first)
         arrived += [m[:3] for m in moves]
         token = after(token, *(s.blocks[k, j] for s, k, j, _ in moves), *values)
 
     if scatters:
         order = [(p, j) for p in range(pairs) for j in range(n_y)]
         rest = [key for key in order if key not in made]
+        sent = send(rest, (token,))[1] if rest else ()
+        waiting = [key for key in order if key not in rest and ("piece",) + key not in v]
+        if waiting:
+            keep(waiting, (token,) + sent)
+        place([key for key in order if key not in rest])
         if rest:
-            scatter(rest, (token,))
-        out = hidden
-        for p, j in sorted(order, key=lambda key: key in rest):
-            for c, (kept, came) in enumerate(v["piece", p, j]):
-                first = (((z_at - p) % pairs) * n_y + (y_at + j) % n_y) * n_core
-                first = (first + (core_at + c) % n_core) * o_cols
-                branch = kept.astype(jnp.float32) + came.astype(jnp.float32)
-                here = lax.dynamic_slice(hidden, (0, first), (tok_rows, o_cols)).astype(jnp.float32)
-                out = lax.dynamic_update_slice(out, (here + branch).astype(jnp.bfloat16), (0, first))
-        return out
+            keep(rest, sent)
+            place(rest)
+        return v["mixed"]
 
     made = []
     attn = jnp.concatenate(v["attn"], axis=0)

time: 223 us -> 213 us (0.955)
  other arithmetic: 9.85 us -> 5.6 us
  local copies, waits for them, and re-layouts: 39.3 us -> 35.9 us
  waiting for transfers between devices: 82.3 us -> 79.2 us
    dynamic_update_slice x8 -> x4, other arithmetic: 7.74 us -> 1.01 us  [place(): lax.dynamic_update_slice(v['mixed'], (here + branch).astype(jnp.bfloat16)...]
    ppermute x20 -> x22, waiting for transfers between devices: 69.1 us -> 65.3 us  [swap(): return lax.ppermute(value, axis, pairs)]
    unnamed x97 -> x93, local copies, waits for them, and re-layouts: 34.1 us -> 30.7 us
    select_n x1 -> x4, other arithmetic: 0.13 us -> 2.6 us  [ordered(): jnp.where(flag, first, second)]
    pallas_call x4 -> x5, Pallas kernels: 14.3 us -> 13 us  [out_products(): pl.pallas_call(functools.partial(out_kernel, len(attns), [[len(b) for b i...]
    ppermute x20 -> x22, starting transfers between devices: 14.8 us -> 15.9 us  [swap(): return lax.ppermute(value, axis, pairs)]
  transfers between devices with their start and end apart: 28 -> 30, of which waited for: 13 -> 16; matrix products, arithmetic and copies ran while one was open for 6% -> 5% of each run, Pallas kernels for 26% -> 27%
where the time goes in v3:
time: 213 us
  waiting for transfers between devices  79.2 us (37%)
  Pallas kernels  62.9 us (30%)
  local copies, waits for them, and re-layouts  35.9 us (17%)
  starting transfers between devices  28.4 us (13%)
  other arithmetic  5.6 us (3%)
    ppermute x22, waiting for transfers between devices, swap(): return lax.ppermute(value, axis, pairs)  65.3 us
    unnamed x93, local copies, waits for them, and re-layouts  30.7 us
    pallas_call x3, Pallas kernels, project(): pl.pallas_call(functools.partial(project_kernel, len(parts)), in_specs=[W...  16.4 us
    ppermute x22, starting transfers between devices, swap(): return lax.ppermute(value, axis, pairs)  15.9 us
    ppermute x7, waiting for transfers between devices, ring(): lax.ppermute(value, axis, [(i, (i + stride) % count) for i in range(count)])  13.9 us
    pallas_call x5, Pallas kernels, out_products(): pl.pallas_call(functools.partial(out_kernel, len(attns), [[len(b) for b i...  13 us
    pallas_call x3, Pallas kernels, add_query(): pl.pallas_call(functools.partial(query_kernel, len(norms), len(blocks), l...  11.3 us
    pallas_call x2, Pallas kernels, encode_partial(): pl.pallas_call(encode_kernel, in_specs=[WHOLE] * 4, out_specs=WHOLE, out_...  10.5 us
  transfers between devices with their start and end apart: 30, of which 16 were waited for; matrix products, arithmetic and copies ran while one was open for 5% of the time, Pallas kernels for 27%

profile of v3, /device:TPU:0, one launch (start us, length us, event | category | flops | bytes accessed | tf_op | source)
XLA Modules:
  0.0 212.6 jit_solution(15668689417447422751)
XLA Ops:
  0.0 3.0 %collective-permute-start.5 = (bf16[2048,256]{1,0:T(8,128)(2,1)}, bf16[2048,256]{1,0:T(8,128)(2,1)S(1)}, u32[]{:S(2)}, u32[]{:S(2)}) collective-permute-start(bf16[2048,256]{1,0:T(8,128)(2,1)} %refs_2_.5), channel_id=1, source_target_pairs={{0,4},{2,6},{4,0},{6,2},{8,12},{10,14},{12,8},{14,10},{16,20},{18,... | collective-permute-start | bytes 3145736 | tf_op jit(solution)/shard_map/out_0_1/ppermute | solution.py:24
  3.0 1.4 constant_dynamic-slice_fusion.1
  4.5 1.6 collective-permute-start
  6.1 2.7 %fusion.12 = (bf16[2,256,896]{2,1,0:T(8,128)(2,1)}, bf16[2,256,896]{2,1,0:T(8,128)(2,1)S(1)}) fusion(bf16[4,256,896]{2,1,0:T(8,128)(2,1)} %param.13), kind=kLoop, calls=%fused_computation.48 | loop fusion | bytes 3670016 | tf_op jit(solution)/shard_map/slice | solution.py:345
  8.8 1.6 collective-permute-start.2
  11.0 2.2 %collective-permute-start.4 = (bf16[512,1024]{1,0:T(8,128)(2,1)S(1)}, bf16[512,1024]{1,0:T(8,128)(2,1)}, u32[]{:S(2)}, u32[]{:S(2)}) collective-permute-start(bf16[512,1024]{1,0:T(8,128)(2,1)S(1)} %pad_maximum_fusion.refs_2_), channel_id=1, source_target_pairs={{0,24},{2,26},{4,28},{6,30},{8,0},{10,2},{12,4},{14,6},{16,8},{18,... | collective-permute-start | bytes 3145736 | tf_op jit(solution)/shard_map/query_3_0/ppermute | solution.py:29
  13.2 5.3 %encode.2.refs_1_ = bf16[512,896]{1,0:T(8,128)(2,1)} custom-call(bf16[512,896]{1,0:T(8,128)(2,1)S(1)} %bitcast.39, f32[1,896]{1,0:T(1,128)S(1)} %reshape.56.gain_ref, bf16[896,1792]{1,0:T(8,128)(2,1)S(1)} %copy-done.36, bf16[1792,896]{1,0:T(8,128)(2,1)S(1)} %copy-done.38), custom_call_target="tpu_custom_call" | custom-call | flops 3288334336 | bytes 6422528 | tf_op jit(solution)/shard_map/encode/encode/pallas_call | solution.py:104
  18.5 8.7 %collective-permute-done.5.refs_4_.refs_2_ = bf16[2048,256]{1,0:T(8,128)(2,1)S(1)} collective-permute-done((bf16[2048,256]{1,0:T(8,128)(2,1)}, bf16[2048,256]{1,0:T(8,128)(2,1)S(1)}, u32[]{:S(2)}, u32[]{:S(2)}) %collective-permute-start.5) | collective-permute-done | bytes 1048608 | tf_op jit(solution)/shard_map/out_0_1/ppermute | solution.py:24
  27.2 2.0 collective-permute-start.6
  29.2 1.2 copy-done.30
  30.4 1.9 copy-done.37
  32.3 1.9 copy-done.39
  34.2 5.2 %encode.3.refs_1_ = bf16[512,896]{1,0:T(8,128)(2,1)} custom-call(bf16[512,896]{1,0:T(8,128)(2,1)S(1)} %bitcast.37, f32[1,896]{1,0:T(1,128)S(1)} %reshape.56.gain_ref, bf16[896,1792]{1,0:T(8,128)(2,1)S(1)} %copy-done.37, bf16[1792,896]{1,0:T(8,128)(2,1)S(1)} %copy-done.39), custom_call_target="tpu_custom_call" | custom-call | flops 3288334336 | bytes 6422528 | tf_op jit(solution)/shard_map/encode/encode/pallas_call | solution.py:104
  39.4 10.4 %collective-permute-done.6.refs_2_ = bf16[512,896]{1,0:T(8,128)(2,1)} collective-permute-done((bf16[512,896]{1,0:T(8,128)(2,1)}, bf16[512,896]{1,0:T(8,128)(2,1)}, u32[]{:S(2)}, u32[]{:S(2)}) %collective-permute-start.6) | collective-permute-done | bytes 917536 | tf_op jit(solution)/shard_map/encode_sum/ppermute | solution.py:24
  49.8 8.4 %collective-permute-done.4.refs_5_ = bf16[512,1024]{1,0:T(8,128)(2,1)} collective-permute-done((bf16[512,1024]{1,0:T(8,128)(2,1)S(1)}, bf16[512,1024]{1,0:T(8,128)(2,1)}, u32[]{:S(2)}, u32[]{:S(2)}) %collective-permute-start.4) | collective-permute-done | bytes 1048608 | tf_op jit(solution)/shard_map/query_3_0/ppermute | solution.py:29
  58.2 2.4 %decode.1.refs_0_ = bf16[16,256,256]{2,1,0:T(8,128)(2,1)S(1)} custom-call(s32[2]{0:T(128)S(1)} %broadcast_select_fusion.2.at_ref, bf16[256,2048]{1,0:T(8,128)(2,1)S(1)} %copy-done.5, bf16[256,2048]{1,0:T(8,128)(2,1)} %collective-permute-done.came_ref, f32[16,1,256]{2,1,0:T(1,128)S(1)} %bitcast.41), custom_call_target="tpu_custom_call" | custom-call | bytes 5242880 | tf_op jit(solution)/shard_map/decode/decode/pallas_call | solution.py:172
  60.7 1.0 collective-permute-start.7
  62.1 1.5 collective-permute-start.10
  64.8 1.3 copy-done
  66.7 2.0 copy-done.16
  68.8 2.0 copy-done.19
  70.8 1.2 copy-done.33
  72.0 6.1 %project.3 = (bf16[512,896]{1,0:T(8,128)(2,1)}, bf16[512,2048]{1,0:T(8,128)(2,1)S(1)}, bf16[512,2048]{1,0:T(8,128)(2,1)S(1)}) custom-call(bf16[512,896]{1,0:T(8,128)(2,1)S(1)} %bitcast.40, bf16[512,896]{1,0:T(8,128)(2,1)} %encode.2.refs_1_, bf16[512,896]{1,0:T(8,128)(2,1)} %collective-permute-done.6.refs_2_, bf16[896,2048]{1,0:T(8,128)(2,1)S(1)} %copy-done.16, ...), custom_call_target="tpu_custom_call" | custom-call | flops 3758096384 | bytes 7340032 | tf_op jit(solution)/shard_map/keys_values/project/pallas_call | solution.py:140
  78.2 5.7 %query.3.refs_5_ = f32[512,1024]{1,0:T(8,128)S(1)} custom-call(s32[8]{0:T(128)S(1)} %stack.96.at_ref, bf16[16,256,256]{2,1,0:T(8,128)(2,1)S(1)} %decode.1.refs_0_, bf16[16,256,256]{2,1,0:T(8,128)(2,1)S(1)} %copy-done.1, bf16[512,1024]{1,0:T(8,128)(2,1)S(1)} %copy-done.15, bf16[512,1024]{1,0:T(8,128)(2,1)} %collective-permute-done.2.refs_3_, ...), custom_call_target="tpu_custom_call" | custom-call | flops 2147483648 | bytes 4194304 | tf_op jit(solution)/shard_map/query_part/query/pallas_call | solution.py:210
  83.9 1.4 copy-done.3
  85.3 24.3 %collective-permute-done.10.refs_4_ = bf16[512,1024]{1,0:T(8,128)(2,1)} collective-permute-done((bf16[512,1024]{1,0:T(8,128)(2,1)}, bf16[512,1024]{1,0:T(8,128)(2,1)}, u32[]{:S(2)}, u32[]{:S(2)}) %collective-permute-start.10) | collective-permute-done | bytes 1048608 | tf_op jit(solution)/shard_map/query_3_1/ppermute | solution.py:24
  109.6 1.2 collective-permute-done.9.refs_4_.refs_6_
  111.8 2.0 copy-done.17
  113.9 2.0 copy-done.20
  115.9 1.2 copy-done.31
  117.1 6.1 %project.4 = (bf16[512,896]{1,0:T(8,128)(2,1)S(1)}, bf16[512,2048]{1,0:T(8,128)(2,1)S(1)}, bf16[512,2048]{1,0:T(8,128)(2,1)S(1)}) custom-call(bf16[512,896]{1,0:T(8,128)(2,1)S(1)} %bitcast.38, bf16[512,896]{1,0:T(8,128)(2,1)} %encode.3.refs_1_, bf16[512,896]{1,0:T(8,128)(2,1)} %collective-permute-done.12.refs_2_, bf16[896,2048]{1,0:T(8,128)(2,1)S(1)} %copy-done.17, ...), custom_call_target="tpu_custom_call" | custom-call | flops 3758096384 | bytes 7340032 | tf_op jit(solution)/shard_map/keys_values/project/pallas_call | solution.py:140
  123.2 1.3 copy-done.26
  125.4 2.1 collective-permute-start.16
  127.5 3.7 %query.4.refs_3_ = f32[512,1024]{1,0:T(8,128)S(1)} custom-call(s32[6]{0:T(128)S(1)} %stack.103.at_ref, bf16[16,256,256]{2,1,0:T(8,128)(2,1)S(1)} %decode.1.refs_0_, bf16[16,256,256]{2,1,0:T(8,128)(2,1)S(1)} %copy-done.2, bf16[512,1024]{1,0:T(8,128)(2,1)} %collective-permute-done.7.refs_2_, bf16[512,1024]{1,0:T(8,128)(2,1)} %collective-permute-done.8.refs_3_, ...), custom_call_target="tpu_custom_call" | custom-call | flops 1610612736 | bytes 3145728 | tf_op jit(solution)/shard_map/query_part/query/pallas_call | solution.py:210
  131.2 4.7 %collective-permute-done.14.refs_2_ = bf16[512,1024]{1,0:T(8,128)(2,1)} collective-permute-done((bf16[512,1024]{1,0:T(8,128)(2,1)}, bf16[512,1024]{1,0:T(8,128)(2,1)}, u32[]{:S(2)}, u32[]{:S(2)}) %collective-permute-start.14) | collective-permute-done | bytes 1048608 | tf_op jit(solution)/shard_map/query_2_1/ppermute | solution.py:24
  135.9 2.4 %collective-permute-done.13.refs_3_ = bf16[2048,256]{1,0:T(8,128)(2,1)} collective-permute-done((bf16[2048,256]{1,0:T(8,128)(2,1)}, bf16[2048,256]{1,0:T(8,128)(2,1)}, u32[]{:S(2)}, u32[]{:S(2)}) %collective-permute-start.13) | collective-permute-done | bytes 1048608 | tf_op jit(solution)/shard_map/out_2_0/ppermute | solution.py:29
  138.2 1.9 query.5
  140.2 1.0 copy-done.12
  141.3 1.2 collective-permute-start.18
  142.5 1.7 collective-permute-start.17
  144.2 2.0 copy-done.18
  146.3 2.0 copy-done.21
  148.3 4.1 %project.5 = (bf16[256,896]{1,0:T(8,128)(2,1)}, bf16[256,2048]{1,0:T(8,128)(2,1)S(1)}, bf16[256,2048]{1,0:T(8,128)(2,1)S(1)}) custom-call(bf16[256,896]{1,0:T(8,128)(2,1)} %collective-permute-done.16.refs_0_, bf16[896,2048]{1,0:T(8,128)(2,1)S(1)} %copy-done.18, bf16[896,2048]{1,0:T(8,128)(2,1)S(1)} %copy-done.21), custom_call_target="tpu_custom_call" | custom-call | flops 1879048192 | bytes 7340032 | tf_op jit(solution)/shard_map/keys_values_earlier/project/pallas_call | solution.py:140
  152.8 1.1 copy-done.23
  154.6 9.5 %attend.1 = bf16[320,2048]{1,0:T(8,128)(2,1)S(1)} custom-call(bf16[320,2048]{1,0:T(8,128)(2,1)S(1)} %fusion.3.q_ref, bf16[256,2048]{1,0:T(8,128)(2,1)S(1)} %get-tuple-element.91.refs_0_, bf16[512,2048]{1,0:T(8,128)(2,1)S(1)} %copy-done.23, bf16[512,2048]{1,0:T(8,128)(2,1)S(1)} %copy-done.27, bf16[256,2048]{1,0:T(8,128)(2,1)S(1)} %get-tuple-element.92.refs_3_, ...), custom_call_target="tpu_custom_call" | custom-call | bytes 1024 | tf_op jit(solution)/shard_map/attention/attend/pallas_call | solution.py:294
  164.6 2.5 %collective-permute-done.18.refs_5_.refs_3_ = bf16[2048,256]{1,0:T(8,128)(2,1)} collective-permute-done((bf16[2048,256]{1,0:T(8,128)(2,1)}, bf16[2048,256]{1,0:T(8,128)(2,1)}, u32[]{:S(2)}, u32[]{:S(2)}) %collective-permute-start.18) | collective-permute-done | bytes 1048608 | tf_op jit(solution)/shard_map/out_2_1/ppermute | solution.py:24
  168.1 3.6 %out.5 = (bf16[2,256,256]{2,1,0:T(8,128)(2,1)S(1)}, bf16[2,256,256]{2,1,0:T(8,128)(2,1)S(1)}) custom-call(s32[2]{0:T(128)S(1)} %add_subtract_fusion.near_ref, bf16[256,2048]{1,0:T(8,128)(2,1)S(1)} %slice_select_fusion.refs_0_, bf16[256,2048]{1,0:T(8,128)(2,1)S(1)} %collective-permute-done.19.refs_1_, bf16[2048,256]{1,0:T(8,128)(2,1)} %refs_2_.5, ...), custom_call_target="tpu_custom_call" | custom-call | bytes 1024 | tf_op jit(solution)/shard_map/send/out/pallas_call | solution.py:249
  171.8 0.9 collective-permute-start.26
  172.7 3.2 %collective-permute-start.25 = (bf16[2048,256]{1,0:T(8,128)(2,1)S(1)}, bf16[2048,256]{1,0:T(8,128)(2,1)S(1)}, u32[]{:S(2)}, u32[]{:S(2)}) collective-permute-start(bf16[2048,256]{1,0:T(8,128)(2,1)S(1)} %copy-done.7), channel_id=1, source_target_pairs={{0,24},{2,26},{4,28},{6,30},{8,0},{10,2},{12,4},{14,6},{16,8},{18,... | collective-permute-start | bytes 3145736 | tf_op jit(solution)/shard_map/out_3_1/ppermute | solution.py:29
  176.6 1.9 out.7
  178.6 1.3 collective-permute-done.23
  179.9 1.6 collective-permute-start.24
  181.6 9.4 %collective-permute-done.21 = bf16[4,256,256]{2,1,0:T(8,128)(2,1)} collective-permute-done((bf16[4,256,256]{2,1,0:T(8,128)(2,1)S(1)}, bf16[4,256,256]{2,1,0:T(8,128)(2,1)}, u32[]{:S(2)}, u32[]{:S(2)}) %collective-permute-start.21) | collective-permute-done | bytes 524320 | tf_op jit(solution)/shard_map/send/ppermute | solution.py:24
  190.9 5.4 %out.6 = (bf16[3,256,256]{2,1,0:T(8,128)(2,1)S(1)}, bf16[3,256,256]{2,1,0:T(8,128)(2,1)}) custom-call(s32[3]{0:T(128)S(1)} %pad_add_fusion.near_ref, bf16[256,2048]{1,0:T(8,128)(2,1)S(1)} %slice_select_fusion.refs_0_, bf16[256,2048]{1,0:T(8,128)(2,1)S(1)} %collective-permute-done.19.refs_1_, bf16[2048,256]{1,0:T(8,128)(2,1)} %refs_2_.5, ...), custom_call_target="tpu_custom_call" | custom-call | bytes 1024 | tf_op jit(solution)/shard_map/keep/out/pallas_call | solution.py:249
  196.4 1.2 collective-permute-done.26.refs_2_
  197.6 1.1 collective-permute-done.25.refs_3_
  198.6 1.3 out.8
  200.7 1.0 copy.13
  202.3 1.0 pad_maximum_fusion.3
  203.9 1.2 copy-done.9
  205.2 1.2 copy-done.11
  207.3 1.1 select_bitcast_fusion.5
  208.4 1.3 select_bitcast_fusion.3
  210.0 1.7 collective-permute-done.28
  (130 shorter events, 12.4 us)
Async XLA Ops:
  0.0 4.5 %copy-start.5 = (bf16[256,2048]{1,0:T(8,128)(2,1)S(1)}, bf16[256,2048]{1,0:T(8,128)(2,1)}, u32[]{:S(2)}) copy-start(bf16[256,2048]{1,0:T(8,128)(2,1)} %own_ref.1) | copy-start | bytes 3145732
  0.0 6.0 %copy-start.44 = (f32[896]{0:T(1024)S(1)}, f32[896]{0:T(1024)}, u32[]{:S(2)}) copy-start(f32[896]{0:T(1024)} %param.14) | copy-start | bytes 10756
  0.0 27.2 %collective-permute-start.5 = (bf16[2048,256]{1,0:T(8,128)(2,1)}, bf16[2048,256]{1,0:T(8,128)(2,1)S(1)}, u32[]{:S(2)}, u32[]{:S(2)}) collective-permute-start(bf16[2048,256]{1,0:T(8,128)(2,1)} %refs_2_.5), channel_id=1, source_target_pairs={{0,4},{2,6},{4,0},{6,2},{8,12},{10,14},{12,8},{14,10},{16,20},{18,... | collective-permute-start | bytes 3145736 | tf_op jit(solution)/shard_map/out_0_1/ppermute | solution.py:24
  3.0 10.3 %copy-start.38 = (bf16[1792,896]{1,0:T(8,128)(2,1)S(1)}, bf16[1792,896]{1,0:T(8,128)(2,1)}, u32[]{:S(2)}) copy-start(bf16[1792,896]{1,0:T(8,128)(2,1)} %second_ref.3) | copy-start | bytes 9633796
  4.4 4.4 %collective-permute-start.1 = (bf16[256,1024]{1,0:T(8,128)(2,1)S(1)}, bf16[256,1024]{1,0:T(8,128)(2,1)S(1)}, u32[]{:S(2)}, u32[]{:S(2)}) collective-permute-start(bf16[256,1024]{1,0:T(8,128)(2,1)S(1)} %get-tuple-element.128), channel_id=1, source_target_pairs={{0,2},{2,0},{4,6},{6,4},{8,10},{10,8},{12,14},{14,12},{16,18},{18,... | collective-permute-start | bytes 1572872 | tf_op jit(solution)/shard_map/ppermute | solution.py:24
  4.5 35.0 %collective-permute-start = (bf16[256,2048]{1,0:T(8,128)(2,1)S(1)}, bf16[256,2048]{1,0:T(8,128)(2,1)}, u32[]{:S(2)}, u32[]{:S(2)}) collective-permute-start(bf16[256,2048]{1,0:T(8,128)(2,1)S(1)} %copy-done.5), channel_id=1, source_target_pairs={{0,1},{1,0},{2,3},{3,2},{4,5},{5,4},{6,7},{7,6},{8,9},{9,8},{10,11... | collective-permute-start | bytes 3145736 | tf_op jit(solution)/shard_map/ppermute | solution.py:24
  6.0 7.2 %copy-start.36 = (bf16[896,1792]{1,0:T(8,128)(2,1)S(1)}, bf16[896,1792]{1,0:T(8,128)(2,1)}, u32[]{:S(2)}) copy-start(bf16[896,1792]{1,0:T(8,128)(2,1)} %first_ref.3) | copy-start | bytes 9633796
  8.8 9.7 %copy-start.32 = (bf16[2,256,896]{2,1,0:T(8,128)(2,1)}, bf16[2,256,896]{2,1,0:T(8,128)(2,1)S(1)}, u32[]{:S(2)}) copy-start(bf16[2,256,896]{2,1,0:T(8,128)(2,1)S(1)} %get-tuple-element.118) | copy-start | bytes 2752516
  8.8 9.7 %copy-start.14 = (bf16[512,1024]{1,0:T(8,128)(2,1)}, bf16[512,1024]{1,0:T(8,128)(2,1)S(1)}, u32[]{:S(2)}) copy-start(bf16[512,1024]{1,0:T(8,128)(2,1)S(1)} %pad_maximum_fusion.refs_2_) | copy-start | bytes 3145732
  8.8 41.0 %collective-permute-start.2 = (bf16[512,1024]{1,0:T(8,128)(2,1)S(1)}, bf16[512,1024]{1,0:T(8,128)(2,1)}, u32[]{:S(2)}, u32[]{:S(2)}) collective-permute-start(bf16[512,1024]{1,0:T(8,128)(2,1)S(1)} %pad_maximum_fusion.refs_2_), channel_id=1, source_target_pairs={{0,8},{2,10},{4,12},{6,14},{8,16},{10,18},{12,20},{14,22},{16,24},... | collective-permute-start | bytes 3145736 | tf_op jit(solution)/shard_map/query_1_0/ppermute | solution.py:29
  10.5 39.4 %collective-permute-start.3 = (bf16[512,1024]{1,0:T(8,128)(2,1)S(1)}, bf16[512,1024]{1,0:T(8,128)(2,1)}, u32[]{:S(2)}, u32[]{:S(2)}) collective-permute-start(bf16[512,1024]{1,0:T(8,128)(2,1)S(1)} %pad_maximum_fusion.refs_2_), channel_id=1, source_target_pairs={{0,4},{2,6},{4,0},{6,2},{8,12},{10,14},{12,8},{14,10},{16,20},{18,... | collective-permute-start | bytes 3145736 | tf_op jit(solution)/shard_map/query_0_1/ppermute | solution.py:24
  11.0 47.2 %collective-permute-start.4 = (bf16[512,1024]{1,0:T(8,128)(2,1)S(1)}, bf16[512,1024]{1,0:T(8,128)(2,1)}, u32[]{:S(2)}, u32[]{:S(2)}) collective-permute-start(bf16[512,1024]{1,0:T(8,128)(2,1)S(1)} %pad_maximum_fusion.refs_2_), channel_id=1, source_target_pairs={{0,24},{2,26},{4,28},{6,30},{8,0},{10,2},{12,4},{14,6},{16,8},{18,... | collective-permute-start | bytes 3145736 | tf_op jit(solution)/shard_map/query_3_0/ppermute | solution.py:29
  13.2 16.0 %copy-start.45 = (s32[2]{0:T(128)S(1)}, s32[2]{0:T(128)}, u32[]{:S(2)}) copy-start(s32[2]{0:T(128)} %constant.259.clone) | copy-start | bytes 28
  27.2 12.3 %copy-start.6 = (bf16[2048,256]{1,0:T(8,128)(2,1)}, bf16[2048,256]{1,0:T(8,128)(2,1)S(1)}, u32[]{:S(2)}) copy-start(bf16[2048,256]{1,0:T(8,128)(2,1)S(1)} %collective-permute-done.5.refs_4_.refs_2_) | copy-start | bytes 3145732
  27.2 22.7 %collective-permute-start.6 = (bf16[512,896]{1,0:T(8,128)(2,1)}, bf16[512,896]{1,0:T(8,128)(2,1)}, u32[]{:S(2)}, u32[]{:S(2)}) collective-permute-start(bf16[512,896]{1,0:T(8,128)(2,1)} %encode.2.refs_1_), channel_id=1, source_target_pairs={{0,1},{1,0},{2,3},{3,2},{4,5},{5,4},{6,7},{7,6},{8,9},{9,8},{10,11... | collective-permute-start | bytes 2752520 | tf_op jit(solution)/shard_map/encode_sum/ppermute | solution.py:24
  30.4 1.9 copy-start.37
  32.3 1.9 copy-start.39
  34.2 24.0 %copy-start.35 = (f32[4096]{0:T(1024)S(1)}, f32[4096]{0:T(1024)}, u32[]{:S(2)}) copy-start(f32[4096]{0:T(1024)} %param.19) | copy-start | bytes 49156
  60.6 4.2 %collective-permute-start.11 = (bf16[16,256,256]{2,1,0:T(8,128)(2,1)S(1)}, bf16[16,256,256]{2,1,0:T(8,128)(2,1)S(1)}, u32[]{:S(2)}, u32[]{:S(2)}) collective-permute-start(bf16[16,256,256]{2,1,0:T(8,128)(2,1)S(1)} %decode.1.refs_0_), channel_id=1, source_target_pairs={{0,2},{2,0},{4,6},{6,4},{8,10},{10,8},{12,14},{14,12},{16,18},{18,... | collective-permute-start | bytes 6291464 | tf_op jit(solution)/shard_map/decode/ppermute | solution.py:24
  60.7 49.0 %collective-permute-start.7 = (bf16[512,1024]{1,0:T(8,128)(2,1)}, bf16[512,1024]{1,0:T(8,128)(2,1)}, u32[]{:S(2)}, u32[]{:S(2)}) collective-permute-start(bf16[512,1024]{1,0:T(8,128)(2,1)} %collective-permute-done.2.refs_3_), channel_id=1, source_target_pairs={{0,8},{2,10},{4,12},{6,14},{8,16},{10,18},{12,20},{14,22},{16,24},... | collective-permute-start | bytes 3145736 | tf_op jit(solution)/shard_map/query_2_0/ppermute | solution.py:29
  61.6 48.0 %collective-permute-start.8 = (bf16[512,1024]{1,0:T(8,128)(2,1)}, bf16[512,1024]{1,0:T(8,128)(2,1)}, u32[]{:S(2)}, u32[]{:S(2)}) collective-permute-start(bf16[512,1024]{1,0:T(8,128)(2,1)} %collective-permute-done.2.refs_3_), channel_id=1, source_target_pairs={{0,4},{2,6},{4,0},{6,2},{8,12},{10,14},{12,8},{14,10},{16,20},{18,... | collective-permute-start | bytes 3145736 | tf_op jit(solution)/shard_map/query_1_1/ppermute | solution.py:24
  62.1 47.5 %collective-permute-start.10 = (bf16[512,1024]{1,0:T(8,128)(2,1)}, bf16[512,1024]{1,0:T(8,128)(2,1)}, u32[]{:S(2)}, u32[]{:S(2)}) collective-permute-start(bf16[512,1024]{1,0:T(8,128)(2,1)} %collective-permute-done.4.refs_5_), channel_id=1, source_target_pairs={{0,4},{2,6},{4,0},{6,2},{8,12},{10,14},{12,8},{14,10},{16,20},{18,... | collective-permute-start | bytes 3145736 | tf_op jit(solution)/shard_map/query_3_1/ppermute | solution.py:24
  63.7 47.1 %collective-permute-start.9 = (bf16[2048,256]{1,0:T(8,128)(2,1)}, bf16[2048,256]{1,0:T(8,128)(2,1)}, u32[]{:S(2)}, u32[]{:S(2)}) collective-permute-start(bf16[2048,256]{1,0:T(8,128)(2,1)} %refs_2_.5), channel_id=1, source_target_pairs={{0,8},{2,10},{4,12},{6,14},{8,16},{10,18},{12,20},{14,22},{16,24},... | collective-permute-start | bytes 3145736 | tf_op jit(solution)/shard_map/out_1_0/ppermute | solution.py:29
  66.1 44.7 %collective-permute-start.12 = (bf16[512,896]{1,0:T(8,128)(2,1)}, bf16[512,896]{1,0:T(8,128)(2,1)}, u32[]{:S(2)}, u32[]{:S(2)}) collective-permute-start(bf16[512,896]{1,0:T(8,128)(2,1)} %encode.3.refs_1_), channel_id=1, source_target_pairs={{0,1},{1,0},{2,3},{3,2},{4,5},{5,4},{6,7},{7,6},{8,9},{9,8},{10,11... | collective-permute-start | bytes 2752520 | tf_op jit(solution)/shard_map/encode_sum/ppermute | solution.py:24
  66.7 2.0 copy-start.16
  68.8 2.0 copy-start.19
  72.0 6.2 %copy-start.1 = (bf16[16,256,256]{2,1,0:T(8,128)(2,1)S(1)}, bf16[16,256,256]{2,1,0:T(8,128)(2,1)}, u32[]{:S(2)}) copy-start(bf16[16,256,256]{2,1,0:T(8,128)(2,1)} %copy-done) | copy-start | bytes 6291460
  72.0 6.2 %copy-start.15 = (bf16[512,1024]{1,0:T(8,128)(2,1)S(1)}, bf16[512,1024]{1,0:T(8,128)(2,1)}, u32[]{:S(2)}) copy-start(bf16[512,1024]{1,0:T(8,128)(2,1)} %copy-done.14) | copy-start | bytes 3145732
  78.2 5.7 %copy-start.22 = (bf16[512,2048]{1,0:T(8,128)(2,1)}, bf16[512,2048]{1,0:T(8,128)(2,1)S(1)}, u32[]{:S(2)}) copy-start(bf16[512,2048]{1,0:T(8,128)(2,1)S(1)} %get-tuple-element.72.refs_1_) | copy-start | bytes 6291460
  78.2 5.7 %copy-start.24 = (bf16[512,2048]{1,0:T(8,128)(2,1)}, bf16[512,2048]{1,0:T(8,128)(2,1)S(1)}, u32[]{:S(2)}) copy-start(bf16[512,2048]{1,0:T(8,128)(2,1)S(1)} %get-tuple-element.73.refs_4_) | copy-start | bytes 6291460
  110.8 25.0 %collective-permute-start.14 = (bf16[512,1024]{1,0:T(8,128)(2,1)}, bf16[512,1024]{1,0:T(8,128)(2,1)}, u32[]{:S(2)}, u32[]{:S(2)}) collective-permute-start(bf16[512,1024]{1,0:T(8,128)(2,1)} %collective-permute-done.7.refs_2_), channel_id=1, source_target_pairs={{0,4},{2,6},{4,0},{6,2},{8,12},{10,14},{12,8},{14,10},{16,20},{18,... | collective-permute-start | bytes 3145736 | tf_op jit(solution)/shard_map/query_2_1/ppermute | solution.py:24
  111.7 26.6 %collective-permute-start.13 = (bf16[2048,256]{1,0:T(8,128)(2,1)}, bf16[2048,256]{1,0:T(8,128)(2,1)}, u32[]{:S(2)}, u32[]{:S(2)}) collective-permute-start(bf16[2048,256]{1,0:T(8,128)(2,1)} %collective-permute-done.9.refs_4_.refs_6_), channel_id=1, source_target_pairs={{0,8},{2,10},{4,12},{6,14},{8,16},{10,18},{12,20},{14,22},{16,24},... | collective-permute-start | bytes 3145736 | tf_op jit(solution)/shard_map/out_2_0/ppermute | solution.py:29
  111.8 2.0 copy-start.17
  113.9 2.0 copy-start.20
  117.1 10.4 %copy-start.2 = (bf16[16,256,256]{2,1,0:T(8,128)(2,1)S(1)}, bf16[16,256,256]{2,1,0:T(8,128)(2,1)}, u32[]{:S(2)}) copy-start(bf16[16,256,256]{2,1,0:T(8,128)(2,1)} %copy-done) | copy-start | bytes 6291460
  117.1 10.4 %copy-start.4 = (f32[512,1024]{1,0:T(8,128)S(1)}, f32[512,1024]{1,0:T(8,128)}, u32[]{:S(2)}) copy-start(f32[512,1024]{1,0:T(8,128)} %copy-done.3) | copy-start | bytes 6291460
  124.6 6.6 %copy-start.28 = (bf16[512,2048]{1,0:T(8,128)(2,1)}, bf16[512,2048]{1,0:T(8,128)(2,1)S(1)}, u32[]{:S(2)}) copy-start(bf16[512,2048]{1,0:T(8,128)(2,1)S(1)} %get-tuple-element.83.refs_5_) | copy-start | bytes 6291460
  125.4 17.1 %collective-permute-start.16 = (bf16[256,896]{1,0:T(8,128)(2,1)}, bf16[256,896]{1,0:T(8,128)(2,1)}, u32[]{:S(2)}, u32[]{:S(2)}) collective-permute-start(bf16[256,896]{1,0:T(8,128)(2,1)} %slice.72), channel_id=1, source_target_pairs={{0,2},{2,4},{4,6},{6,8},{8,10},{10,12},{12,14},{14,16},{16,18},{18... | collective-permute-start | bytes 1376264 | tf_op jit(solution)/shard_map/keys_values/ppermute | solution.py:381
  141.2 11.2 %collective-permute-start.15 = (bf16[256,1024]{1,0:T(8,128)(2,1)S(1)}, bf16[256,1024]{1,0:T(8,128)(2,1)S(1)}, u32[]{:S(2)}, u32[]{:S(2)}) collective-permute-start(bf16[256,1024]{1,0:T(8,128)(2,1)S(1)} %slice.89), channel_id=1, source_target_pairs={{0,2},{2,0},{4,6},{6,4},{8,10},{10,8},{12,14},{14,12},{16,18},{18,... | collective-permute-start | bytes 1572872 | tf_op jit(solution)/shard_map/attention/ppermute | solution.py:24
  141.3 11.1 %copy-start.13 = (bf16[512,1024]{1,0:T(8,128)(2,1)S(1)}, bf16[512,1024]{1,0:T(8,128)(2,1)}, u32[]{:S(2)}) copy-start(bf16[512,1024]{1,0:T(8,128)(2,1)} %copy-done.12) | copy-start | bytes 3145732
  141.3 25.9 %collective-permute-start.18 = (bf16[2048,256]{1,0:T(8,128)(2,1)}, bf16[2048,256]{1,0:T(8,128)(2,1)}, u32[]{:S(2)}, u32[]{:S(2)}) collective-permute-start(bf16[2048,256]{1,0:T(8,128)(2,1)} %collective-permute-done.13.refs_3_), channel_id=1, source_target_pairs={{0,4},{2,6},{4,0},{6,2},{8,12},{10,14},{12,8},{14,10},{16,20},{18,... | collective-permute-start | bytes 3145736 | tf_op jit(solution)/shard_map/out_2_1/ppermute | solution.py:24
  142.5 25.5 %collective-permute-start.17 = (bf16[2048,256]{1,0:T(8,128)(2,1)}, bf16[2048,256]{1,0:T(8,128)(2,1)}, u32[]{:S(2)}, u32[]{:S(2)}) collective-permute-start(bf16[2048,256]{1,0:T(8,128)(2,1)} %refs_2_.5), channel_id=1, source_target_pairs={{0,24},{2,26},{4,28},{6,30},{8,0},{10,2},{12,4},{14,6},{16,8},{18,... | collective-permute-start | bytes 3145736 | tf_op jit(solution)/shard_map/out_3_0/ppermute | solution.py:29
  144.2 2.0 copy-start.18
  146.3 2.0 copy-start.21
  148.3 4.5 %copy-start.27 = (bf16[512,2048]{1,0:T(8,128)(2,1)S(1)}, bf16[512,2048]{1,0:T(8,128)(2,1)}, u32[]{:S(2)}) copy-start(bf16[512,2048]{1,0:T(8,128)(2,1)} %copy-done.26) | copy-start | bytes 6291460
  148.3 4.5 %copy-start.29 = (bf16[512,2048]{1,0:T(8,128)(2,1)S(1)}, bf16[512,2048]{1,0:T(8,128)(2,1)}, u32[]{:S(2)}) copy-start(bf16[512,2048]{1,0:T(8,128)(2,1)} %copy-done.28) | copy-start | bytes 6291460
  152.4 1.6 copy-start.23
  152.4 2.2 %copy-start.25 = (bf16[512,2048]{1,0:T(8,128)(2,1)S(1)}, bf16[512,2048]{1,0:T(8,128)(2,1)}, u32[]{:S(2)}) copy-start(bf16[512,2048]{1,0:T(8,128)(2,1)} %copy-done.24) | copy-start | bytes 6291460
  164.4 3.7 %collective-permute-start.19 = (bf16[256,2048]{1,0:T(8,128)(2,1)S(1)}, bf16[256,2048]{1,0:T(8,128)(2,1)S(1)}, u32[]{:S(2)}, u32[]{:S(2)}) collective-permute-start(bf16[256,2048]{1,0:T(8,128)(2,1)S(1)} %slice_select_fusion.refs_0_), channel_id=1, source_target_pairs={{0,2},{2,0},{4,6},{6,4},{8,10},{10,8},{12,14},{14,12},{16,18},{18,... | collective-permute-start | bytes 3145736 | tf_op jit(solution)/shard_map/attention/ppermute | solution.py:24
  164.6 8.1 %copy-start.7 = (bf16[2048,256]{1,0:T(8,128)(2,1)S(1)}, bf16[2048,256]{1,0:T(8,128)(2,1)}, u32[]{:S(2)}) copy-start(bf16[2048,256]{1,0:T(8,128)(2,1)} %copy-done.6) | copy-start | bytes 3145732
  171.7 4.2 %collective-permute-start.20 = (bf16[2,256,256]{2,1,0:T(8,128)(2,1)S(1)}, bf16[2,256,256]{2,1,0:T(8,128)(2,1)S(1)}, u32[]{:S(2)}, u32[]{:S(2)}) collective-permute-start(bf16[2,256,256]{2,1,0:T(8,128)(2,1)S(1)} %get-tuple-element.99), channel_id=1, source_target_pairs={{0,2},{2,0},{4,6},{6,4},{8,10},{10,8},{12,14},{14,12},{16,18},{18,... | collective-permute-start | bytes 786440 | tf_op jit(solution)/shard_map/send/ppermute | solution.py:24
  171.8 25.8 %collective-permute-start.26 = (bf16[2048,256]{1,0:T(8,128)(2,1)}, bf16[2048,256]{1,0:T(8,128)(2,1)S(1)}, u32[]{:S(2)}, u32[]{:S(2)}) collective-permute-start(bf16[2048,256]{1,0:T(8,128)(2,1)} %collective-permute-done.9.refs_4_.refs_6_), channel_id=1, source_target_pairs={{0,4},{2,6},{4,0},{6,2},{8,12},{10,14},{12,8},{14,10},{16,20},{18,... | collective-permute-start | bytes 3145736 | tf_op jit(solution)/shard_map/out_1_1/ppermute | solution.py:24
  172.7 26.0 %collective-permute-start.25 = (bf16[2048,256]{1,0:T(8,128)(2,1)S(1)}, bf16[2048,256]{1,0:T(8,128)(2,1)S(1)}, u32[]{:S(2)}, u32[]{:S(2)}) collective-permute-start(bf16[2048,256]{1,0:T(8,128)(2,1)S(1)} %copy-done.7), channel_id=1, source_target_pairs={{0,24},{2,26},{4,28},{6,30},{8,0},{10,2},{12,4},{14,6},{16,8},{18,... | collective-permute-start | bytes 3145736 | tf_op jit(solution)/shard_map/out_3_1/ppermute | solution.py:29
  176.0 15.0 %collective-permute-start.21 = (bf16[4,256,256]{2,1,0:T(8,128)(2,1)S(1)}, bf16[4,256,256]{2,1,0:T(8,128)(2,1)}, u32[]{:S(2)}, u32[]{:S(2)}) collective-permute-start(bf16[4,256,256]{2,1,0:T(8,128)(2,1)S(1)} %pad_maximum_fusion.1), channel_id=1, source_target_pairs={{0,1},{1,0},{2,3},{3,2},{4,5},{5,4},{6,7},{7,6},{8,9},{9,8},{10,11... | collective-permute-start | bytes 1572872 | tf_op jit(solution)/shard_map/send/ppermute | solution.py:24
  178.5 1.4 collective-permute-start.23
  179.9 16.4 %collective-permute-start.24 = (bf16[2,256,256]{2,1,0:T(8,128)(2,1)S(1)}, bf16[2,256,256]{2,1,0:T(8,128)(2,1)S(1)}, u32[]{:S(2)}, u32[]{:S(2)}) collective-permute-start(bf16[2,256,256]{2,1,0:T(8,128)(2,1)S(1)} %pad_maximum_fusion.2), channel_id=1, source_target_pairs={{0,1},{1,0},{2,3},{3,2},{4,5},{5,4},{6,7},{7,6},{8,9},{9,8},{10,11... | collective-permute-start | bytes 786440 | tf_op jit(solution)/shard_map/send/ppermute | solution.py:24
  196.3 10.9 %collective-permute-start.22 = (bf16[3,256,256]{2,1,0:T(8,128)(2,1)}, bf16[3,256,256]{2,1,0:T(8,128)(2,1)}, u32[]{:S(2)}, u32[]{:S(2)}) collective-permute-start(bf16[3,256,256]{2,1,0:T(8,128)(2,1)} %get-tuple-element.103), channel_id=1, source_target_pairs={{0,2},{2,0},{4,6},{6,4},{8,10},{10,8},{12,14},{14,12},{16,18},{18,... | collective-permute-start | bytes 1179656 | tf_op jit(solution)/shard_map/keep/ppermute | solution.py:24
  196.4 3.6 %copy-start.42 = (bf16[2,256,256]{2,1,0:T(8,128)(2,1)}, bf16[2,256,256]{2,1,0:T(8,128)(2,1)S(1)}, u32[]{:S(2)}) copy-start(bf16[2,256,256]{2,1,0:T(8,128)(2,1)S(1)} %collective-permute-done.24) | copy-start | bytes 786436
  197.6 2.4 %copy-start.8 = (bf16[2048,256]{1,0:T(8,128)(2,1)}, bf16[2048,256]{1,0:T(8,128)(2,1)S(1)}, u32[]{:S(2)}) copy-start(bf16[2048,256]{1,0:T(8,128)(2,1)S(1)} %collective-permute-done.26.refs_2_) | copy-start | bytes 3145732
  200.7 1.7 collective-permute-start.27
  203.3 8.4 %collective-permute-start.28 = (bf16[2,256,256]{2,1,0:T(8,128)(2,1)S(1)}, bf16[2,256,256]{2,1,0:T(8,128)(2,1)S(1)}, u32[]{:S(2)}, u32[]{:S(2)}) collective-permute-start(bf16[2,256,256]{2,1,0:T(8,128)(2,1)S(1)} %pad_maximum_fusion.3), channel_id=1, source_target_pairs={{0,1},{1,0},{2,3},{3,2},{4,5},{5,4},{6,7},{7,6},{8,9},{9,8},{10,11... | collective-permute-start | bytes 786440 | tf_op jit(solution)/shard_map/send/ppermute | solution.py:24
  207.1 2.6 %copy-start.40 = (bf16[256,2048]{1,0:T(8,128)(2,1)S(1)}, bf16[256,2048]{1,0:T(8,128)(2,1)}, u32[]{:S(2)}) copy-start(bf16[256,2048]{1,0:T(8,128)(2,1)} %copy.13) | copy-start | bytes 3145732
  207.1 2.9 %collective-permute-start.29 = (bf16[1,256,256]{2,1,0:T(8,128)(2,1)S(1)}, bf16[1,256,256]{2,1,0:T(8,128)(2,1)S(1)}, u32[]{:S(2)}, u32[]{:S(2)}) collective-permute-start(bf16[1,256,256]{2,1,0:T(8,128)(2,1)S(1)} %get-tuple-element.116), channel_id=1, source_target_pairs={{0,2},{2,0},{4,6},{6,4},{8,10},{10,8},{12,14},{14,12},{16,18},{18,... | collective-permute-start | bytes 393224 | tf_op jit(solution)/shard_map/keep/ppermute | solution.py:24
  210.0 1.8 copy-start.41
  (12 other events, 14.0 us)
